TPU v7x, 128 devices: a whole 4x4x4 slice. The times are simulated.
128 devices in a mesh: user: 32 (over y, x, core), item: 4 (over z).
Axes of the slice: x: 4, y: 4, z: 4, core: 2. Of those that a mesh axis runs over, the one named last changes fastest.
Arguments:
- user_emb: bfloat16 [32, 1024, 256], P('user'), may hold values from -6 to 6
- item_emb: bfloat16 [32, 4, 128, 256], P('user', 'item'), may hold values from -6 to 6
- user_degree: int32 [32, 1024], P('user'), may hold values from 16 to 160
- item_degree: int32 [32, 4, 128], P('user', 'item'), may hold values from 16 to 160
- tiles: int32 [32, 4, 64, 128, 128], P('user', 'item'), may hold values 0 or 1
- tile_user: int32 [32, 4, 64], P('user', 'item'), may hold values from 0 to 7
- tile_item: int32 [32, 4, 64], P('user', 'item'), may hold values from 0 to 31
- tile_count: int32 [32, 4], P('user', 'item'), may hold values from 8 to 64, as said below
- triple_user: int32 [32, 4, 256], P('user', 'item'), may hold values from 0 to 1023
- triple_pos: int32 [32, 4, 256], P('user', 'item'), may hold values from 0 to 4095
- triple_neg: int32 [32, 4, 256], P('user', 'item'), may hold values from 0 to 4095
Outputs:
- grad_user: float32 [32, 1024, 256], P('user')
- grad_item: float32 [32, 4, 128, 256], P('user', 'item')
Inputs may be any that keep to these rules, and one draw needn't show every extreme that they name: Slots 0 to tile_count[a, c] - 1 of tiles[a, c] are live, the others are not part of R; in every draw some device has all 64 slots live.
All inputs are finite; a program needn't handle non-finite values. No bound on the sum of `tiles` on one device may be relied on, other than what follows from the above.
Results may differ from a plain program's by a relative error of at most 0.006.
Values may be sent and summed in bfloat16 or wider, within the bound.
A program may use at most 128 MiB of HBM per device.

v0:
```python
import jax
import jax.numpy as jnp
from jax import lax
from jax.sharding import PartitionSpec as P

LAYERS = 2


def per_device(
    user_emb,
    item_emb,
    user_degree,
    item_degree,
    tiles,
    tile_user,
    tile_item,
    tile_count,
    triple_user,
    triple_pos,
    triple_neg,
):
    slots = tiles.shape[2]
    block = tiles.shape[-1]
    rows_u = user_emb.shape[1]
    rows_i = item_emb.shape[2]
    width = user_emb.shape[2]
    col_rows = rows_i * lax.axis_size("user")
    col_blocks = col_rows // block
    user_blocks = rows_u // block
    user_scale = lax.rsqrt(user_degree[0].astype(jnp.float32))[:, None]
    live = (jnp.arange(slots) < tile_count[0, 0]).astype(jnp.bfloat16)
    tile_mats = tiles[0, 0].astype(jnp.bfloat16) * live[:, None, None]
    tile_rows = tile_user[0, 0]
    tile_cols = tile_item[0, 0]

    def user_side(feed_col):
        picked = feed_col.reshape(col_blocks, block, width)[tile_cols]
        prods = jnp.einsum("tuv,tvd->tud", tile_mats, picked, preferred_element_type=jnp.float32)
        return jax.ops.segment_sum(prods, tile_rows, num_segments=user_blocks).reshape(
            rows_u, width
        )

    def item_terms(feed_user):
        picked = feed_user.reshape(user_blocks, block, width)[tile_rows]
        prods = jnp.einsum("tuv,tud->tvd", tile_mats, picked, preferred_element_type=jnp.float32)
        column_sums = jax.ops.segment_sum(prods, tile_cols, num_segments=col_blocks).reshape(
            col_rows, width
        )

        def term(start, count):
            return column_sums

        return term

    item_scale = lax.rsqrt(item_degree[0, 0].astype(jnp.float32))[:, None]
    item_first = item_emb[0, 0]

    def spread(feed):
        return lax.all_gather(feed, "user", axis=0, tiled=True)

    def settle(term):
        return lax.psum_scatter(
            term(jnp.int32(0), lax.axis_size("user") * rows_i),
            "user",
            scatter_dimension=0,
            tiled=True,
        )

    def total_users(part):
        return lax.psum(part, "item")

    def propagate(feed_user, feed_item):
        column = spread(feed_item)
        user_part = user_side(column)
        term = item_terms(feed_user)
        item_sum = settle(term)
        return (total_users(user_part), item_sum)

    user_state = user_emb[0]
    item_state = item_first
    user_total = user_state.astype(jnp.float32)
    item_total = item_state.astype(jnp.float32)
    for layer in range(LAYERS):
        feed_user = (user_scale * user_state.astype(jnp.float32)).astype(jnp.bfloat16)
        feed_item = (item_scale * item_state.astype(jnp.float32)).astype(jnp.bfloat16)
        user_sum, item_sum = propagate(feed_user, feed_item)
        user_state = (user_scale * user_sum).astype(jnp.bfloat16)
        item_state = (item_scale * item_sum).astype(jnp.bfloat16)
        user_total = user_total + user_state.astype(jnp.float32)
        item_total = item_total + item_state.astype(jnp.float32)
    final_user = (user_total / (LAYERS + 1.0)).astype(jnp.bfloat16)
    final_item = spread((item_total / (LAYERS + 1.0)).astype(jnp.bfloat16))
    chosen_users = triple_user[0, 0]
    chosen_pos = triple_pos[0, 0]
    chosen_neg = triple_neg[0, 0]
    user_rows = final_user[chosen_users].astype(jnp.float32)
    diff = final_item[chosen_pos].astype(jnp.float32) - final_item[chosen_neg].astype(jnp.float32)
    score = jnp.sum(user_rows * diff, axis=1)
    weight = jax.nn.sigmoid(-score)[:, None]
    user_grad_part = jnp.zeros((rows_u, width), jnp.float32).at[chosen_users].add(-weight * diff)
    item_grad_col = (
        jnp.zeros((col_rows, width), jnp.float32).at[chosen_pos].add(-weight * user_rows)
    )
    item_grad_col = item_grad_col.at[chosen_neg].add(weight * user_rows)

    def grad_term(start, count):
        return item_grad_col

    grad_u = total_users(user_grad_part)
    grad_i = settle(grad_term)
    carry_user, carry_item = (grad_u, grad_i)
    for layer in range(LAYERS):
        feed_user = (user_scale * carry_user).astype(jnp.bfloat16)
        feed_item = (item_scale * carry_item).astype(jnp.bfloat16)
        user_sum, item_sum = propagate(feed_user, feed_item)
        carry_user = grad_u + user_scale * user_sum
        carry_item = grad_i + item_scale * item_sum
    grad_user = carry_user / (LAYERS + 1.0)
    grad_item = carry_item / (LAYERS + 1.0)
    return (grad_user[None], grad_item[None, None])


def solution(mesh):
    return jax.shard_map(
        per_device,
        mesh=mesh,
        in_specs=(
            P("user", None, None),
            P("user", "item", None, None),
            P("user", None),
            P("user", "item", None),
            P("user", "item", None, None, None),
            P("user", "item", None),
            P("user", "item", None),
            P("user", "item"),
            P("user", "item", None),
            P("user", "item", None),
            P("user", "item", None),
        ),
        out_specs=(P("user", None, None), P("user", "item", None, None)),
        check_vma=False,
    )
```

profile of v0, /device:TPU:0, one launch (start us, length us, event | category | flops | bytes accessed | tf_op | source)
XLA Modules:
  0.0 1025.2 jit_solution(15578503202319264252)
XLA Ops:
  14.8 6.7 fusion.23
  24.0 18.9 %scatter_fusion.1 = f32[32,128,256]{2,1,0:T(8,128)} fusion(f32[32,128,256]{2,1,0:T(8,128)} %broadcast.133.clone.1, s32[64]{0:T(128)S(1)} %bitcast.94, f32[64,128,256]{2,1,0:T(8,128)} %fusion.23), kind=kCustom, calls=%fused_computation.12 | custom fusion | flops 2097152 | bytes 25166080 | tf_op jit(solution)/shard_map/scatter-add | solution.py:46
  43.5 83.8 %reduce-scatter.6.cloned.1.call-done = f32[128,256]{1,0:T(8,128)} async-done(((f32[4096,256]{1,0:T(8,128)}), f32[128,256]{1,0:T(8,128)}) %reduce-scatter.6.cloned.1.call-update) | async-done | bytes 131088 | tf_op jit(solution)/shard_map/reduce_scatter | solution.py:62
  129.8 43.7 %all-gather.6.cloned.1.call-done = bf16[4096,256]{1,0:T(8,128)(2,1)} async-done(((bf16[128,256]{1,0:T(8,128)(2,1)}), bf16[4096,256]{1,0:T(8,128)(2,1)}) %all-gather.6.cloned.1.call-update) | async-done | bytes 2097168 | tf_op jit(solution)/shard_map/all_gather | solution.py:59
  184.5 35.1 %all-gather.8.cloned.1.call-done = bf16[4096,256]{1,0:T(8,128)(2,1)} async-done(((bf16[128,256]{1,0:T(8,128)(2,1)}), bf16[4096,256]{1,0:T(8,128)(2,1)}) %all-gather.8.cloned.1.call-update) | async-done | bytes 2097168 | tf_op jit(solution)/shard_map/all_gather | solution.py:59
  230.7 12.4 %scatter_fusion = f32[8,128,256]{2,1,0:T(8,128)S(1)} fusion(f32[8,128,256]{2,1,0:T(8,128)S(1)} %broadcast.130.clone, s32[64]{0:T(128)S(1)} %bitcast.90, f32[64,128,256]{2,1,0:T(8,128)} %fusion.22), kind=kCustom, calls=%fused_computation.11 | custom fusion | flops 2097152 | bytes 25166080 | tf_op jit(solution)/shard_map/scatter-add | solution.py:39
  244.2 18.5 %scatter_fusion.2 = f32[8,128,256]{2,1,0:T(8,128)} fusion(f32[8,128,256]{2,1,0:T(8,128)} %broadcast.130.clone.1, s32[64]{0:T(128)S(1)} %bitcast.91, f32[64,128,256]{2,1,0:T(8,128)} %fusion.24), kind=kCustom, calls=%fused_computation.13 | custom fusion | flops 2097152 | bytes 25166080 | tf_op jit(solution)/shard_map/scatter-add | solution.py:39
  263.0 58.5 %all-reduce.10.cloned.1.call-done = (f32[1024,256]{1,0:T(8,128)}, f32[1024,256]{1,0:T(8,128)}) async-done(((f32[1024,256]{1,0:T(8,128)}, f32[1024,256]{1,0:T(8,128)}), (f32[1024,256]{1,0:T(8,128)}, f32[1024,256]{1,0:T(8,128)})) %all-reduce.10.cloned.1.call-update) | async-done | bytes 2097168 | tf_op jit(solution)/shard_map/psum | solution.py:70
  326.3 6.7 fusion.25
  335.5 18.9 %scatter_fusion.3 = f32[32,128,256]{2,1,0:T(8,128)} fusion(f32[32,128,256]{2,1,0:T(8,128)} %broadcast.133.clone, s32[64]{0:T(128)S(1)} %bitcast.95, f32[64,128,256]{2,1,0:T(8,128)} %fusion.25), kind=kCustom, calls=%fused_computation.14 | custom fusion | flops 2097152 | bytes 25166080 | tf_op jit(solution)/shard_map/scatter-add | solution.py:46
  354.4 81.7 %reduce-scatter.8.cloned.1.call-done = f32[128,256]{1,0:T(8,128)} async-done(((f32[4096,256]{1,0:T(8,128)}), f32[128,256]{1,0:T(8,128)}) %reduce-scatter.8.cloned.1.call-update) | async-done | bytes 131088 | tf_op jit(solution)/shard_map/reduce_scatter | solution.py:62
  439.1 43.1 %all-gather.10.cloned.1.call-done = bf16[4096,256]{1,0:T(8,128)(2,1)} async-done(((bf16[128,256]{1,0:T(8,128)(2,1)}), bf16[4096,256]{1,0:T(8,128)(2,1)}) %all-gather.10.cloned.1.call-update) | async-done | bytes 2097168 | tf_op jit(solution)/shard_map/all_gather | solution.py:59
  501.6 35.0 %all-reduce.6.cloned.1.call-done = f32[1024,256]{1,0:T(8,128)} async-done(((f32[1024,256]{1,0:T(8,128)}), f32[1024,256]{1,0:T(8,128)}) %all-reduce.6.cloned.1.call-update) | async-done | bytes 1048592 | tf_op jit(solution)/shard_map/psum | solution.py:70
  550.0 19.4 %scatter_fusion.4 = f32[32,128,256]{2,1,0:T(8,128)} fusion(f32[32,128,256]{2,1,0:T(8,128)} %broadcast.133.clone.2, s32[64]{0:T(128)S(1)} %bitcast.96, f32[64,128,256]{2,1,0:T(8,128)} %fusion.26), kind=kCustom, calls=%fused_computation.18 | custom fusion | flops 2097152 | bytes 25166080 | tf_op jit(solution)/shard_map/scatter-add | solution.py:46
  569.4 53.3 %reduce-scatter.10.cloned.1.call-done = f32[128,256]{1,0:T(8,128)} async-done(((f32[4096,256]{1,0:T(8,128)}), f32[128,256]{1,0:T(8,128)}) %reduce-scatter.10.cloned.1.call-update) | async-done | bytes 131088 | tf_op jit(solution)/shard_map/reduce_scatter | solution.py:62
  622.7 85.3 %reduce-scatter.12.cloned.1.call-done = f32[128,256]{1,0:T(8,128)} async-done(((f32[4096,256]{1,0:T(8,128)}), f32[128,256]{1,0:T(8,128)}) %reduce-scatter.12.cloned.1.call-update) | async-done | bytes 131088 | tf_op jit(solution)/shard_map/reduce_scatter | solution.py:62
  710.6 43.3 %all-gather.14.cloned.1.call-done = bf16[4096,256]{1,0:T(8,128)(2,1)} async-done(((bf16[128,256]{1,0:T(8,128)(2,1)}), bf16[4096,256]{1,0:T(8,128)(2,1)}) %all-gather.14.cloned.1.call-update) | async-done | bytes 2097168 | tf_op jit(solution)/shard_map/all_gather | solution.py:59
  764.9 34.8 %all-gather.12.cloned.1.call-done = bf16[4096,256]{1,0:T(8,128)(2,1)} async-done(((bf16[128,256]{1,0:T(8,128)(2,1)}), bf16[4096,256]{1,0:T(8,128)(2,1)}) %all-gather.12.cloned.1.call-update) | async-done | bytes 2097168 | tf_op jit(solution)/shard_map/all_gather | solution.py:59
  810.8 12.4 %scatter_fusion.6 = f32[8,128,256]{2,1,0:T(8,128)S(1)} fusion(f32[8,128,256]{2,1,0:T(8,128)S(1)} %broadcast.130.clone.3, s32[64]{0:T(128)S(1)} %bitcast.92, f32[64,128,256]{2,1,0:T(8,128)} %fusion.28), kind=kCustom, calls=%fused_computation.20 | custom fusion | flops 2097152 | bytes 25166080 | tf_op jit(solution)/shard_map/scatter-add | solution.py:39
  824.3 18.3 %scatter_fusion.5 = f32[8,128,256]{2,1,0:T(8,128)} fusion(f32[8,128,256]{2,1,0:T(8,128)} %broadcast.130.clone.2, s32[64]{0:T(128)S(1)} %bitcast.93, f32[64,128,256]{2,1,0:T(8,128)} %fusion.27), kind=kCustom, calls=%fused_computation.19 | custom fusion | flops 2097152 | bytes 25166080 | tf_op jit(solution)/shard_map/scatter-add | solution.py:39
  843.0 58.4 %all-reduce.8.cloned.1.call-done = (f32[1024,256]{1,0:T(8,128)}, f32[1024,256]{1,0:T(8,128)}) async-done(((f32[1024,256]{1,0:T(8,128)}, f32[1024,256]{1,0:T(8,128)}), (f32[1024,256]{1,0:T(8,128)}, f32[1024,256]{1,0:T(8,128)})) %all-reduce.8.cloned.1.call-update) | async-done | bytes 2097168 | tf_op jit(solution)/shard_map/psum | solution.py:70
  907.2 6.7 fusion.29
  916.4 18.9 %scatter_fusion.7 = f32[32,128,256]{2,1,0:T(8,128)} fusion(f32[32,128,256]{2,1,0:T(8,128)} %broadcast.133, s32[64]{0:T(128)S(1)} %bitcast.97, f32[64,128,256]{2,1,0:T(8,128)} %fusion.29), kind=kCustom, calls=%fused_computation.21 | custom fusion | flops 2097152 | bytes 25166080 | tf_op jit(solution)/shard_map/scatter-add | solution.py:46
  935.3 81.7 %reduce-scatter.14.cloned.1.call-done = f32[128,256]{1,0:T(8,128)} async-done(((f32[4096,256]{1,0:T(8,128)}), f32[128,256]{1,0:T(8,128)}) %reduce-scatter.14.cloned.1.call-update) | async-done | bytes 131088 | tf_op jit(solution)/shard_map/reduce_scatter | solution.py:62
  (101 shorter events, 115.1 us)
Async XLA Ops:
  7.2 4.6 copy-start.2
  7.2 120.1 %reduce-scatter.6.cloned.1.call-start = ((), (), s32[]{:S(2)}) async-start(), calls=%async_computation.6 | async-start | bytes 4325376 | tf_op jit(solution)/shard_map/reduce_scatter | solution.py:62
  21.5 2.5 copy-start.7
  42.8 84.5 %copy-start.5 = (bf16[1,1,128,256]{3,2,1,0:T(8,128)(2,1)S(1)}, bf16[1,1,128,256]{3,2,1,0:T(8,128)(2,1)}, u32[]{:S(2)}) copy-start(bf16[1,1,128,256]{3,2,1,0:T(8,128)(2,1)} %param.12) | copy-start | bytes 196612
  42.9 130.6 %all-gather.6.cloned.1.call-start = ((), (), s32[]{:S(2)}) async-start(), calls=%async_computation.5 | async-start | bytes 2162688 | tf_op jit(solution)/shard_map/all_gather | solution.py:59
  129.0 90.6 %all-gather.8.cloned.1.call-start = ((), (), s32[]{:S(2)}) async-start(), calls=%async_computation.7 | async-start | bytes 2162688 | tf_op jit(solution)/shard_map/all_gather | solution.py:59
  129.7 191.8 %all-reduce.10.cloned.1.call-start = ((), (), s32[]{:S(2)}) async-start(), calls=%async_computation.17 | async-start | bytes 4194304 | tf_op jit(solution)/shard_map/psum | solution.py:70
  223.9 6.7 copy-start.6
  243.0 19.7 %copy-start = (f32[8,128,256]{2,1,0:T(8,128)}, f32[8,128,256]{2,1,0:T(8,128)S(1)}, u32[]{:S(2)}) copy-start(f32[8,128,256]{2,1,0:T(8,128)S(1)} %scatter_fusion) | copy-start | bytes 3145732
  262.8 173.4 %reduce-scatter.8.cloned.1.call-start = ((), (), s32[]{:S(2)}) async-start(), calls=%async_computation.8 | async-start | bytes 4325376 | tf_op jit(solution)/shard_map/reduce_scatter | solution.py:62
  354.4 81.8 %copy-start.3 = (f32[128,256]{1,0:T(8,128)S(1)}, f32[128,256]{1,0:T(8,128)}, u32[]{:S(2)}) copy-start(f32[128,256]{1,0:T(8,128)} %reduce-scatter.6.cloned.1.call-done) | copy-start | bytes 393220
  354.4 83.5 %copy-start.8 = (s32[1,1,256]{2,1,0:T(1,128)S(1)}, s32[1,1,256]{2,1,0:T(1,128)}, u32[]{:S(2)}) copy-start(s32[1,1,256]{2,1,0:T(1,128)} %param.20) | copy-start | bytes 3076
  354.4 83.5 %copy-start.9 = (s32[1,1,256]{2,1,0:T(1,128)S(1)}, s32[1,1,256]{2,1,0:T(1,128)}, u32[]{:S(2)}) copy-start(s32[1,1,256]{2,1,0:T(1,128)} %param.21) | copy-start | bytes 3076
  354.4 83.5 %copy-start.10 = (s32[1,1,256]{2,1,0:T(1,128)S(1)}, s32[1,1,256]{2,1,0:T(1,128)}, u32[]{:S(2)}) copy-start(s32[1,1,256]{2,1,0:T(1,128)} %param.19) | copy-start | bytes 3076
  354.4 127.8 %all-gather.10.cloned.1.call-start = ((), (), s32[]{:S(2)}) async-start(), calls=%async_computation.9 | async-start | bytes 2162688 | tf_op jit(solution)/shard_map/all_gather | solution.py:59
  437.8 98.8 %all-reduce.6.cloned.1.call-start = ((), (), s32[]{:S(2)}) async-start(), calls=%async_computation.10 | async-start | bytes 2097152 | tf_op jit(solution)/shard_map/psum | solution.py:70
  491.1 131.7 %reduce-scatter.10.cloned.1.call-start = ((), (), s32[]{:S(2)}) async-start(), calls=%async_computation.11 | async-start | bytes 4325376 | tf_op jit(solution)/shard_map/reduce_scatter | solution.py:62
  501.3 206.7 %reduce-scatter.12.cloned.1.call-start = ((), (), s32[]{:S(2)}) async-start(), calls=%async_computation.12 | async-start | bytes 4325376 | tf_op jit(solution)/shard_map/reduce_scatter | solution.py:62
  569.4 184.5 %all-gather.14.cloned.1.call-start = ((), (), s32[]{:S(2)}) async-start(), calls=%async_computation.14 | async-start | bytes 2162688 | tf_op jit(solution)/shard_map/all_gather | solution.py:59
  709.8 89.9 %all-gather.12.cloned.1.call-start = ((), (), s32[]{:S(2)}) async-start(), calls=%async_computation.13 | async-start | bytes 2162688 | tf_op jit(solution)/shard_map/all_gather | solution.py:59
  710.5 190.8 %all-reduce.8.cloned.1.call-start = ((), (), s32[]{:S(2)}) async-start(), calls=%async_computation.16 | async-start | bytes 4194304 | tf_op jit(solution)/shard_map/psum | solution.py:70
  823.1 19.5 %copy-start.1 = (f32[8,128,256]{2,1,0:T(8,128)}, f32[8,128,256]{2,1,0:T(8,128)S(1)}, u32[]{:S(2)}) copy-start(f32[8,128,256]{2,1,0:T(8,128)S(1)} %scatter_fusion.6) | copy-start | bytes 3145732
  842.6 174.4 %reduce-scatter.14.cloned.1.call-start = ((), (), s32[]{:S(2)}) async-start(), calls=%async_computation.15 | async-start | bytes 4325376 | tf_op jit(solution)/shard_map/reduce_scatter | solution.py:62
  935.3 81.8 %copy-start.4 = (f32[128,256]{1,0:T(8,128)S(1)}, f32[128,256]{1,0:T(8,128)}, u32[]{:S(2)}) copy-start(f32[128,256]{1,0:T(8,128)} %reduce-scatter.10.cloned.1.call-done) | copy-start | bytes 393220
  (1 other events, 0.7 us)
Sparse Core Ops, SparseCore 0:
  43.0 84.2 reduce-scatter.5
  130.4 43.0 all-gather.5
  176.6 42.9 all-gather.7
  262.9 58.5 all-reduce.9
  354.5 81.5 reduce-scatter.7
  439.1 43.0 all-gather.9
  491.2 45.3 all-reduce.5
  540.2 82.4 reduce-scatter.9
  626.8 81.1 reduce-scatter.11
  710.7 43.0 all-gather.13
  756.7 42.9 all-gather.11
  842.8 58.5 all-reduce.7
  935.4 81.5 reduce-scatter.13
where the time goes:
time: 1030 us
  waiting for transfers between devices  739 us (72%)
  other arithmetic  168 us (16%)
  matrix products  53.4 us (5%)
  local copies, waits for them, and re-layouts  48.4 us (5%)
  between operations  14.8 us (1%)
    reduce_scatter x5, waiting for transfers between devices, settle(): lax.psum_scatter(term(jnp.int32(0), lax.axis_size('user') * rows_i), 'use...  386 us
    all_gather x5, waiting for transfers between devices, spread(): return lax.all_gather(feed, 'user', axis=0, tiled=True)  200 us
    psum x3, waiting for transfers between devices, total_users(): return lax.psum(part, 'item')  152 us
    scatter-add x4, other arithmetic, item_terms(): jax.ops.segment_sum(prods, tile_cols, num_segments=col_blocks)  76 us
    scatter-add x4, other arithmetic, user_side(): jax.ops.segment_sum(prods, tile_rows, num_segments=user_blocks)  61.5 us
    dot_general x4, matrix products, item_terms(): jnp.einsum('tuv,tud->tvd', tile_mats, picked, preferred_element_type=jnp....  26.8 us
    dot_general x4, matrix products, user_side(): jnp.einsum('tuv,tvd->tud', tile_mats, picked, preferred_element_type=jnp....  26.6 us
  transfers between devices with their start and end apart: 13, of which 13 were waited for; matrix products, arithmetic and copies ran while one was open for 6% of the time, Pallas kernels for 0%

commit v1 on v0

v1 whole, which is shorter than its diff:
```python
import functools

import jax
import jax.numpy as jnp
from jax import lax
from jax.experimental import pallas as pl
from jax.experimental.pallas import tpu as pltpu
from jax.sharding import PartitionSpec as P

F32 = jnp.float32
BF16 = jnp.bfloat16
MESH = pl.DeviceIdType.MESH
SIDE = 4
BLOCK = 128
CHUNK = SIDE * BLOCK


def build_kernel(count_ref, rows_ref, cols_ref, tiles_ref, r_ref, rt_ref):
    zero_rows = 256

    def clear(i, carry):
        at = pl.ds(pl.multiple_of(i * zero_rows, zero_rows), zero_rows)
        r_ref[at, :] = jnp.zeros((zero_rows, r_ref.shape[1]), BF16)
        for j in range(4):
            at = pl.ds(pl.multiple_of((i * 4 + j) * zero_rows, zero_rows), zero_rows)
            rt_ref[at, :] = jnp.zeros((zero_rows, rt_ref.shape[1]), BF16)
        return carry

    lax.fori_loop(0, r_ref.shape[0] // zero_rows, clear, 0)

    def add(slot, carry):
        users = pl.ds(pl.multiple_of(rows_ref[slot] * BLOCK, BLOCK), BLOCK)
        items = pl.ds(pl.multiple_of(cols_ref[slot] * BLOCK, BLOCK), BLOCK)
        tile = tiles_ref[slot].astype(F32)
        r_ref[users, items] = (r_ref[users, items].astype(F32) + tile).astype(BF16)
        rt_ref[items, users] = (rt_ref[items, users].astype(F32) + tile.T).astype(BF16)
        return carry

    lax.fori_loop(0, count_ref[0], add, 0)


def build(count, rows, cols, tiles, users, items):
    smem = pl.BlockSpec(memory_space=pltpu.SMEM)
    vmem = pl.BlockSpec(memory_space=pltpu.VMEM)
    return pl.pallas_call(
        build_kernel,
        out_shape=(
            jax.ShapeDtypeStruct((users, items), BF16),
            jax.ShapeDtypeStruct((items, users), BF16),
        ),
        in_specs=[smem, smem, smem, vmem],
        out_specs=(vmem, vmem),
        compiler_params=pltpu.CompilerParams(vmem_limit_bytes=40 * 2**20),
        name="build",
    )(count, rows, cols, tiles)


def main_kernel(
    user_emb, item_emb, ru, ri, tu_col, tp_col, tn_col, tu_row, tp_row, tn_row, r_hbm, rt_hbm,
    out_user, out_item,
    r_mat, rt_mat, feeds, users, sib_in, sib_out, q_out, q_half, q_full, p_out, p_half, p_full,
    z_out, z_half, z_full, part, upart, user_total, item_total, user_base, item_base, values,
    load_sem, ag_recv, ag_send, rs_recv, rs_send, z_recv, z_send,
):
    a = lax.axis_index("user")
    z = lax.axis_index("item")
    core = a % 2
    x = (a // 2) % SIDE
    y = a // (2 * SIDE)
    p = x + core * (y - x)
    q = y + core * (x - y)
    sibling = a + 1 - 2 * core
    rows_u = user_emb.shape[0]
    quarter = rows_u // SIDE
    half_q = quarter // 2

    def at_pq(pp, qq):
        yy = qq + core * (pp - qq)
        xx = pp + core * (qq - pp)
        return {"user": (yy * SIDE + xx) * 2 + core}

    def turn(i, by):
        return (i + by) % SIDE

    to_p = {1: at_pq(turn(p, 1), q), -1: at_pq(turn(p, 3), q)}
    to_q = {1: at_pq(p, turn(q, 1)), -1: at_pq(p, turn(q, 3))}
    to_z = {1: {"item": turn(z, 1)}, -1: {"item": turn(z, 3)}}
    to_s = {"user": sibling}

    def rows(start, count):
        return pl.ds(pl.multiple_of(start, 64), count)

    def copy(src, dst, send, recv, device):
        return pltpu.make_async_remote_copy(
            src_ref=src, dst_ref=dst, send_sem=send, recv_sem=recv,
            device_id=device, device_id_type=MESH,
        )

    loads = (
        pltpu.make_async_copy(rt_hbm, rt_mat, load_sem.at[0]),
        pltpu.make_async_copy(r_hbm, r_mat, load_sem.at[1]),
    )
    for load in loads:
        load.start()

    barrier = pltpu.get_barrier_semaphore()
    partners = (to_p[1], to_p[-1], to_q[1], to_q[-1], to_z[1], to_z[-1], to_s)
    for device in partners:
        pl.semaphore_signal(barrier, inc=1, device_id=device, device_id_type=MESH)

    def slot(qq, pp, extra=0):
        return ((core * SIDE + qq) * SIDE + pp) * BLOCK + extra

    def gather_copy(r, start, count, device, recv):
        ref = feeds.at[r, rows(start, count)]
        return copy(ref, ref, ag_send.at[r], ag_recv.at[r, recv], device)

    def to_sibling(r, qq, pp):
        gather_copy(r, slot(qq, pp), BLOCK, to_s, 16 + qq).start()

    def spread_block(r, rel):
        pp = turn(p, rel)
        gather_copy(r, slot(q, pp), BLOCK, to_q[1], 4 + rel).start()
        gather_copy(r, slot(q, pp), BLOCK, to_q[-1], 8 + rel).start()
        to_sibling(r, q, pp)

    def gather_start(r):
        gather_copy(r, slot(q, p), BLOCK, to_p[1], 0).start()
        gather_copy(r, slot(q, p), BLOCK, to_p[-1], 1).start()
        spread_block(r, 0)

    def gather_p(r):
        before, after, far = turn(p, 3), turn(p, 1), turn(p, 2)
        gather_copy(r, slot(q, before), BLOCK, to_p[1], 0).wait_recv()
        gather_copy(r, slot(q, before), BLOCK // 2, to_p[1], 2).start()
        spread_block(r, 3)
        gather_copy(r, slot(q, after), BLOCK, to_p[-1], 1).wait_recv()
        gather_copy(r, slot(q, after, BLOCK // 2), BLOCK // 2, to_p[-1], 3).start()
        spread_block(r, 1)

    def gather_far(r):
        far = turn(p, 2)
        gather_copy(r, slot(q, far), BLOCK // 2, to_p[1], 2).wait_recv()
        gather_copy(r, slot(q, far, BLOCK // 2), BLOCK // 2, to_p[-1], 3).wait_recv()
        spread_block(r, 2)

    def gather_q(r):
        for rel in (0, 3, 1, 2):
            pp = turn(p, rel)
            qq = turn(q, 3)
            gather_copy(r, slot(qq, pp), BLOCK, to_q[1], 4 + rel).wait_recv()
            if rel in (0, 2):
                gather_copy(r, slot(qq, pp), BLOCK, to_q[1], 12 + rel).start()
            to_sibling(r, qq, pp)
            qq = turn(q, 1)
            gather_copy(r, slot(qq, pp), BLOCK, to_q[-1], 8 + rel).wait_recv()
            if rel in (1, 3):
                gather_copy(r, slot(qq, pp), BLOCK, to_q[-1], 12 + rel).start()
            to_sibling(r, qq, pp)

    def gather_end(r):
        qq = turn(q, 2)
        for rel in (0, 3, 1, 2):
            pp = turn(p, rel)
            gather_copy(r, slot(qq, pp), BLOCK, to_q[1], 12 + rel).wait_recv()
            to_sibling(r, qq, pp)
        for other in range(SIDE):
            start = ((1 - core) * SIDE + other) * CHUNK
            gather_copy(r, start, CHUNK, to_s, 16 + other).wait_recv()

    def gather_sent(r):
        gather_copy(r, 0, 31 * BLOCK, to_s, 0).wait_send()

    def make_chunk(term, chunk, out_ref):
        def step(i, carry):
            out_ref[rows(i * BLOCK, BLOCK), :] = term(chunk, i).astype(out_ref.dtype)
            return carry

        lax.fori_loop(0, SIDE, step, 0)

    def sum_sibling(r, term):
        def step(j, carry):
            theirs = turn(p, 2 - j + 3 * (j // 2) - 2 * (j // 3))
            make_chunk(term, (1 - core) * SIDE + theirs, sib_out.at[theirs])
            copy(
                sib_out.at[theirs], sib_in.at[r, theirs], rs_send.at[r, 0],
                rs_recv.at[r, theirs], to_s,
            ).start()
            return carry

        lax.fori_loop(0, SIDE, step, 0)

    def own_chunk(r, term, qq):
        make_chunk(term, core * SIDE + qq, part)
        copy(
            sib_out.at[qq], sib_in.at[r, qq], rs_send.at[r, 0], rs_recv.at[r, qq], to_s
        ).wait_recv()
        return part[...] + sib_in[r, qq].astype(F32)

    def q_copy(r, src, dst, recv, device):
        return copy(src, dst, rs_send.at[r, 1], rs_recv.at[r, recv], device)

    def p_copy(r, src, dst, recv, device):
        return copy(src, dst, rs_send.at[r, 2], rs_recv.at[r, recv], device)

    half_c = CHUNK // 2
    half_b = BLOCK // 2

    def sum_q_far(r, term):
        q_out[0] = own_chunk(r, term, turn(q, 2)).astype(BF16)
        q_copy(r, q_out.at[0, :half_c], q_half.at[r, 0], 4, to_q[1]).start()
        q_copy(r, q_out.at[0, half_c:], q_half.at[r, 1], 5, to_q[-1]).start()

    def sum_q_near(r, term):
        value = own_chunk(r, term, turn(q, 1))
        q_out[1, half_c:, :] = value[half_c:].astype(BF16)
        q_copy(r, q_out.at[0, :half_c], q_half.at[r, 0], 4, to_q[1]).wait_recv()
        q_out[1, :half_c, :] = (value[:half_c] + q_half[r, 0].astype(F32)).astype(BF16)
        q_copy(r, q_out.at[1], q_full.at[r, 0], 6, to_q[1]).start()
        value = own_chunk(r, term, turn(q, 3))
        q_out[2, :half_c, :] = value[:half_c].astype(BF16)
        q_copy(r, q_out.at[0, half_c:], q_half.at[r, 1], 5, to_q[-1]).wait_recv()
        q_out[2, half_c:, :] = (value[half_c:] + q_half[r, 1].astype(F32)).astype(BF16)
        q_copy(r, q_out.at[2], q_full.at[r, 1], 7, to_q[-1]).start()

    def sum_q_end(r, term):
        value = own_chunk(r, term, q)
        q_copy(r, q_out.at[1], q_full.at[r, 0], 6, to_q[1]).wait_recv()
        value = value + q_full[r, 0].astype(F32)
        q_copy(r, q_out.at[2], q_full.at[r, 1], 7, to_q[-1]).wait_recv()
        part[...] = value + q_full[r, 1].astype(F32)
        p_out[0] = part[rows(turn(p, 2) * BLOCK, BLOCK), :].astype(BF16)
        p_copy(r, p_out.at[0, :half_b], p_half.at[r, 0], 8, to_p[1]).start()
        p_copy(r, p_out.at[0, half_b:], p_half.at[r, 1], 9, to_p[-1]).start()

    def sum_p_near(r):
        value = part[rows(turn(p, 1) * BLOCK, BLOCK), :]
        p_copy(r, p_out.at[0, :half_b], p_half.at[r, 0], 8, to_p[1]).wait_recv()
        p_out[1, :half_b, :] = (value[:half_b] + p_half[r, 0].astype(F32)).astype(BF16)
        p_out[1, half_b:, :] = value[half_b:].astype(BF16)
        p_copy(r, p_out.at[1], p_full.at[r, 0], 10, to_p[1]).start()
        value = part[rows(turn(p, 3) * BLOCK, BLOCK), :]
        p_copy(r, p_out.at[0, half_b:], p_half.at[r, 1], 9, to_p[-1]).wait_recv()
        p_out[2, half_b:, :] = (value[half_b:] + p_half[r, 1].astype(F32)).astype(BF16)
        p_out[2, :half_b, :] = value[:half_b].astype(BF16)
        p_copy(r, p_out.at[2], p_full.at[r, 1], 11, to_p[-1]).start()

    def sum_p_end(r):
        p_copy(r, p_out.at[1], p_full.at[r, 0], 10, to_p[1]).wait_recv()
        p_copy(r, p_out.at[2], p_full.at[r, 1], 11, to_p[-1]).wait_recv()
        value = part[rows(p * BLOCK, BLOCK), :]
        return value + p_full[r, 0].astype(F32) + p_full[r, 1].astype(F32)

    def sums_sent(r):
        copy(sib_out, sib_in.at[r], rs_send.at[r, 0], rs_recv.at[r, 0], to_s).wait_send()
        q_copy(r, q_out, q_out, 4, to_q[1]).wait_send()
        p_copy(r, p_out, p_out, 8, to_p[1]).wait_send()

    def z_copy(r, src, dst, recv, device):
        return copy(src, dst, z_send.at[r, 0], z_recv.at[r, recv], device)

    def u_copy(r, start, count, recv, device):
        ref = users.at[r + 1, rows(start, count)]
        return copy(ref, ref, z_send.at[r, 1], z_recv.at[r, recv], device)

    def make_users(term):
        def step(i, carry):
            upart[rows(i * BLOCK, BLOCK), :] = term(i)
            return carry

        lax.fori_loop(0, rows_u // BLOCK, step, 0)

    def user_far(r):
        z_out[0] = upart[rows(turn(z, 2) * quarter, quarter), :].astype(BF16)
        z_copy(r, z_out.at[0, :half_q], z_half.at[r, 0], 0, to_z[1]).start()
        z_copy(r, z_out.at[0, half_q:], z_half.at[r, 1], 1, to_z[-1]).start()

    def user_near(r):
        value = upart[rows(turn(z, 1) * quarter, quarter), :]
        z_copy(r, z_out.at[0, :half_q], z_half.at[r, 0], 0, to_z[1]).wait_recv()
        z_out[1, :half_q, :] = (value[:half_q] + z_half[r, 0].astype(F32)).astype(BF16)
        z_out[1, half_q:, :] = value[half_q:].astype(BF16)
        z_copy(r, z_out.at[1], z_full.at[r, 0], 2, to_z[1]).start()
        value = upart[rows(turn(z, 3) * quarter, quarter), :]
        z_copy(r, z_out.at[0, half_q:], z_half.at[r, 1], 1, to_z[-1]).wait_recv()
        z_out[2, half_q:, :] = (value[half_q:] + z_half[r, 1].astype(F32)).astype(BF16)
        z_out[2, :half_q, :] = value[:half_q].astype(BF16)
        z_copy(r, z_out.at[2], z_full.at[r, 1], 3, to_z[-1]).start()

    def user_end(r):
        z_copy(r, z_out.at[1], z_full.at[r, 0], 2, to_z[1]).wait_recv()
        z_copy(r, z_out.at[2], z_full.at[r, 1], 3, to_z[-1]).wait_recv()
        value = upart[rows(z * quarter, quarter), :]
        return value + z_full[r, 0].astype(F32) + z_full[r, 1].astype(F32)

    def user_spread(r, value):
        users[r + 1, rows(z * quarter, quarter), :] = value
        u_copy(r, z * quarter, quarter, 4, to_z[1]).start()
        u_copy(r, z * quarter, quarter, 5, to_z[-1]).start()

    def user_forward(r):
        before, after = turn(z, 3) * quarter, turn(z, 1) * quarter
        u_copy(r, before, quarter, 4, to_z[1]).wait_recv()
        u_copy(r, before, half_q, 6, to_z[1]).start()
        u_copy(r, after, quarter, 5, to_z[-1]).wait_recv()
        u_copy(r, after + half_q, half_q, 7, to_z[-1]).start()

    def user_ready(r):
        far = turn(z, 2) * quarter
        u_copy(r, far, half_q, 6, to_z[1]).wait_recv()
        u_copy(r, far + half_q, half_q, 7, to_z[-1]).wait_recv()

    def users_sent(r):
        z_copy(r, z_out, z_out, 0, to_z[1]).wait_send()
        u_copy(r, 0, 3 * quarter, 4, to_z[1]).wait_send()

    def item_term(r):
        def term(chunk, i):
            mat = rt_mat[rows(chunk * CHUNK + i * BLOCK, BLOCK), :]
            return jnp.dot(mat, users[r], preferred_element_type=F32)

        return term

    def user_term(r):
        def term(i):
            mat = r_mat[rows(i * BLOCK, BLOCK), :]
            return jnp.dot(mat, feeds[r], preferred_element_type=F32)

        return term

    own_u = rows(z * quarter, quarter)
    own_slot = rows(slot(q, p), BLOCK)

    def exchange(r, items, make_user_parts, user_update, item_update, gathering):
        sum_sibling(r, items)
        if gathering:
            gather_p(r)
        sum_q_far(r, items)
        if gathering:
            gather_far(r)
            gather_q(r)
        sum_q_near(r, items)
        if gathering:
            gather_end(r)
        make_user_parts()
        user_far(r)
        sum_q_end(r, items)
        user_near(r)
        sum_p_near(r)
        user_spread(r, user_update(user_end(r)))
        item_update(sum_p_end(r))
        user_forward(r)
        user_ready(r)
        sums_sent(r)
        users_sent(r)
        gather_sent(r)

    eu = user_emb[...].astype(F32)
    users[0] = (ru[...] * eu).astype(BF16)
    ei = item_emb[...].astype(F32)
    feeds[0, own_slot, :] = (ri[...] * ei).astype(BF16)
    user_total[...] = user_emb[own_u, :].astype(F32)
    item_total[...] = ei
    pl.semaphore_wait(barrier, len(partners))
    gather_start(0)
    loads[0].wait()
    loads[1].wait()

    def forward(r, carry):
        def user_update(value):
            state = (ru[own_u, :] * value).astype(BF16).astype(F32)
            user_total[...] += state
            return jnp.where(r == 0, ru[own_u, :] * state, user_total[...] / 3.0).astype(BF16)

        def item_update(value):
            state = (ri[...] * value).astype(BF16).astype(F32)
            item_total[...] += state
            feeds[r + 1, own_slot, :] = jnp.where(
                r == 0, ri[...] * state, item_total[...] / 3.0
            ).astype(BF16)
            gather_start(r + 1)

        exchange(
            r, item_term(r), lambda: make_users(user_term(r)), user_update, item_update, True
        )
        return carry

    lax.fori_loop(0, 2, forward, 0)

    gather_p(2)
    gather_far(2)
    gather_q(2)
    wide = 2 * BLOCK

    def lanes(i, width):
        return i * width + lax.broadcasted_iota(jnp.int32, (wide, width), 1)

    def pick_user(i, carry):
        hot = (tu_col[...] == lanes(i, BLOCK)).astype(F32).astype(BF16)
        values[0] += jnp.dot(hot, users[2, rows(i * BLOCK, BLOCK), :], preferred_element_type=F32)
        return carry

    def pick_item(i, carry):
        spot = lanes(i, BLOCK)
        hot = ((tp_col[...] == spot).astype(F32) - (tn_col[...] == spot).astype(F32)).astype(BF16)
        values[1] += jnp.dot(hot, feeds[2, rows(i * BLOCK, BLOCK), :], preferred_element_type=F32)
        return carry

    values[...] = jnp.zeros_like(values)
    lax.fori_loop(0, rows_u // BLOCK, pick_user, 0)
    gather_end(2)
    lax.fori_loop(0, feeds.shape[1] // BLOCK, pick_item, 0)
    score = jnp.sum(values[0] * values[1], axis=1, keepdims=True)
    weight = jax.nn.sigmoid(-score)
    user_value = -weight * values[1]
    item_value = -weight * values[0]

    def split(value):
        high = value.astype(BF16)
        return high, (value - high.astype(F32)).astype(BF16)

    def spots(start):
        return start + lax.broadcasted_iota(jnp.int32, (BLOCK, wide), 0)

    user_high, user_low = split(user_value)
    item_high, item_low = split(item_value)
    upart_split = (user_high, user_low)
    values_b = (item_high, item_low)

    def grad_item_term(chunk, i):
        spot = spots(chunk * CHUNK + i * BLOCK)
        hot = ((tp_row[...] == spot).astype(F32) - (tn_row[...] == spot).astype(F32)).astype(BF16)
        return sum(jnp.dot(hot, v, preferred_element_type=F32) for v in values_b)

    def grad_user_term(i):
        hot = (tu_row[...] == spots(i * BLOCK)).astype(F32).astype(BF16)
        return sum(jnp.dot(hot, v, preferred_element_type=F32) for v in upart_split)

    def grad_user_update(value):
        user_base[...] = value
        return (ru[own_u, :] * value).astype(BF16)

    def grad_item_update(value):
        item_base[...] = value
        feeds[3, own_slot, :] = (ri[...] * value).astype(BF16)
        gather_start(3)

    exchange(
        2, grad_item_term, lambda: make_users(grad_user_term), grad_user_update,
        grad_item_update, False,
    )

    def backward(r, carry):
        def user_update(value):
            state = user_base[...] + ru[own_u, :] * value
            return jnp.where(r == 3, ru[own_u, :] * state, state / 3.0).astype(BF16)

        def item_update(value):
            state = item_base[...] + ri[...] * value
            out_item[...] = state / 3.0

            @pl.when(r == 3)
            def _():
                feeds[r + 1, own_slot, :] = (ri[...] * state).astype(BF16)
                gather_start(r + 1)

        exchange(
            r, item_term(r), lambda: make_users(user_term(r)), user_update, item_update, True
        )
        return carry

    lax.fori_loop(3, 5, backward, 0)
    out_user[...] = users[5].astype(F32)


def main(user_emb, item_emb, ru, ri, triples, r_hbm, rt_hbm):
    rows_u, width = user_emb.shape
    col_rows = rt_hbm.shape[0]
    rounds = 5
    quarter = rows_u // SIDE
    vmem = pl.BlockSpec(memory_space=pltpu.VMEM)
    hbm = pl.BlockSpec(memory_space=pl.ANY)
    dma = pltpu.SemaphoreType.DMA
    scratch = [
        pltpu.VMEM((rows_u, col_rows), BF16),
        pltpu.VMEM((col_rows, rows_u), BF16),
        pltpu.VMEM((rounds, col_rows, width), BF16),
        pltpu.VMEM((rounds + 1, rows_u, width), BF16),
        pltpu.VMEM((rounds, SIDE, CHUNK, width), BF16),
        pltpu.VMEM((SIDE, CHUNK, width), BF16),
        pltpu.VMEM((3, CHUNK, width), BF16),
        pltpu.VMEM((rounds, 2, CHUNK // 2, width), BF16),
        pltpu.VMEM((rounds, 2, CHUNK, width), BF16),
        pltpu.VMEM((3, BLOCK, width), BF16),
        pltpu.VMEM((rounds, 2, BLOCK // 2, width), BF16),
        pltpu.VMEM((rounds, 2, BLOCK, width), BF16),
        pltpu.VMEM((3, quarter, width), BF16),
        pltpu.VMEM((rounds, 2, quarter // 2, width), BF16),
        pltpu.VMEM((rounds, 2, quarter, width), BF16),
        pltpu.VMEM((CHUNK, width), F32),
        pltpu.VMEM((rows_u, width), F32),
        pltpu.VMEM((quarter, width), F32),
        pltpu.VMEM((BLOCK, width), F32),
        pltpu.VMEM((quarter, width), F32),
        pltpu.VMEM((BLOCK, width), F32),
        pltpu.VMEM((2, 2 * BLOCK, width), F32),
        dma((2,)),
        dma((rounds, 20)),
        dma((rounds,)),
        dma((rounds, 12)),
        dma((rounds, 3)),
        dma((rounds, 8)),
        dma((rounds, 2)),
    ]
    return pl.pallas_call(
        main_kernel,
        out_shape=(
            jax.ShapeDtypeStruct((rows_u, width), F32),
            jax.ShapeDtypeStruct((BLOCK, width), F32),
        ),
        in_specs=[vmem] * 10 + [hbm] * 2,
        out_specs=(vmem, vmem),
        scratch_shapes=scratch,
        compiler_params=pltpu.CompilerParams(
            collective_id=0, has_side_effects=True, vmem_limit_bytes=60 * 2**20
        ),
        name="propagate",
    )(user_emb, item_emb, ru, ri, *triples, r_hbm, rt_hbm)


def place(block):
    core = block % 2
    x = (block // 2) % SIDE
    y = block // (2 * SIDE)
    return core * SIDE * SIDE + jnp.where(core == 0, y * SIDE + x, x * SIDE + y)


def per_device(
    user_emb, item_emb, user_degree, item_degree, tiles, tile_user, tile_item, tile_count,
    triple_user, triple_pos, triple_neg,
):
    rows_u, width = user_emb.shape[1:]
    col_rows = item_emb.shape[2] * lax.axis_size("user")
    r_mat, rt_mat = build(
        tile_count[0], tile_user[0, 0], place(tile_item[0, 0]), tiles[0, 0], rows_u, col_rows
    )
    ru = jnp.broadcast_to(lax.rsqrt(user_degree[0].astype(F32))[:, None], (rows_u, width))
    ri = jnp.broadcast_to(
        lax.rsqrt(item_degree[0, 0].astype(F32))[:, None], (item_emb.shape[2], width)
    )

    def moved(index):
        return place(index // BLOCK) * BLOCK + index % BLOCK

    picks = (triple_user[0, 0], moved(triple_pos[0, 0]), moved(triple_neg[0, 0]))
    columns = tuple(jnp.broadcast_to(v[:, None], (v.shape[0], BLOCK)) for v in picks)
    lines = tuple(v[None, :] for v in picks)
    grad_user, grad_item = main(
        user_emb[0], item_emb[0, 0], ru, ri, columns + lines, r_mat, rt_mat
    )
    return grad_user[None], grad_item[None, None]


def solution(mesh):
    return jax.shard_map(
        per_device,
        mesh=mesh,
        in_specs=(
            P("user", None, None),
            P("user", "item", None, None),
            P("user", None),
            P("user", "item", None),
            P("user", "item", None, None, None),
            P("user", "item", None),
            P("user", "item", None),
            P("user", "item"),
            P("user", "item", None),
            P("user", "item", None),
            P("user", "item", None),
        ),
        out_specs=(P("user", None, None), P("user", "item", None, None)),
        check_vma=False,
    )
```

time: 1030 us -> 243 us (0.24)
  waiting for transfers between devices: 739 us -> 0 us
  Pallas kernels: 0 us -> 220 us
  other arithmetic: 168 us -> 4.77 us
  matrix products: 53.4 us -> 0 us
  local copies, waits for them, and re-layouts: 48.4 us -> 14.7 us
  between operations: 14.8 us -> 1.3 us
    reduce_scatter x5 -> x0, waiting for transfers between devices: 386 us -> none  [settle(): lax.psum_scatter(term(jnp.int32(0), lax.axis_size('user') * rows_i), 'use...]
    pallas_call x0 -> x2, Pallas kernels: none -> 220 us  [the longest x1 212 us: main(): pl.pallas_call(main_kernel, out_shape=(jax.ShapeDtypeStruct((rows_u, widt...]
    all_gather x5 -> x0, waiting for transfers between devices: 200 us -> none  [spread(): return lax.all_gather(feed, 'user', axis=0, tiled=True)]
    psum x3 -> x0, waiting for transfers between devices: 152 us -> none  [total_users(): return lax.psum(part, 'item')]
    scatter-add x11 -> x0, other arithmetic: 151 us -> none  [the longest x4 76 us: item_terms(): jax.ops.segment_sum(prods, tile_cols, num_segments=col_blocks)]
    dot_general x8 -> x0, matrix products: 53.4 us -> none  [the longest x4 26.8 us: item_terms(): jnp.einsum('tuv,tud->tvd', tile_mats, picked, preferred_element_type=jnp....]
    gather x11 -> x0, local copies, waits for them, and re-layouts: 35.4 us -> none  [the longest x4 17.4 us: user_side(): picked = feed_col.reshape(col_blocks, block, width)[tile_cols]]
    another operation x8 -> x0, local copies, waits for them, and re-layouts: 12.4 us -> none
  transfers between devices with their start and end apart: 13 -> 0, of which waited for: 13 -> 0; matrix products, arithmetic and copies ran while one was open for 6% -> 0% of each run, Pallas kernels for 0% -> 0%
where the time goes in v1:
time: 243 us; the launch traced here: 241 us
  Pallas kernels  220 us (91%)
  local copies, waits for them, and re-layouts  14.7 us (6%)
  other arithmetic  4.77 us (2%)
    pallas_call x1, Pallas kernels, main(): pl.pallas_call(main_kernel, out_shape=(jax.ShapeDtypeStruct((rows_u, widt...  212 us
    unnamed x8, local copies, waits for them, and re-layouts  9.88 us
    pallas_call x1, Pallas kernels, build(): pl.pallas_call(build_kernel, out_shape=(jax.ShapeDtypeStruct((users, item...  7.87 us

profile of v1, /device:TPU:0, one launch (start us, length us, event | category | flops | bytes accessed | tf_op | source)
XLA Modules:
  0.0 240.7 jit_solution(8372596116224974609)
XLA Ops:
  1.3 0.7 rsqrt_bitcast_fusion
  1.9 0.7 fusion.14.cols_ref
  2.6 0.7 fusion.7
  3.3 0.7 fusion.4
  4.0 1.3 fusion
  5.4 0.7 convert_rsqrt_fusion
  6.1 0.7 broadcast_in_dim.20.tp_col
  6.8 0.8 broadcast_in_dim.21.tn_col
  7.5 0.7 broadcast_in_dim.17.ri
  8.3 1.4 broadcast_in_dim.19.tu_col
  9.7 1.2 broadcast_in_dim.16.ru
  10.9 0.0 copy-start.1
  10.9 2.2 copy-done.1
  13.1 0.0 copy-start.2
  13.1 0.7 copy-done.2
  13.7 7.9 %build.1 = (bf16[1024,4096]{1,0:T(8,128)(2,1)S(1)}, bf16[4096,1024]{1,0:T(8,128)(2,1)}) custom-call(s32[1]{0:T(128)} %bitcast.56.count_ref, s32[64]{0:T(128)S(1)} %bitcast.58, s32[64]{0:T(128)S(1)} %fusion.14.cols_ref, s32[64,128,128]{2,1,0:T(8,128)S(1)} %bitcast.57), custom_call_target="tpu_custom_call" | custom-call | tf_op jit(solution)/shard_map/build/pallas_call | solution.py:45
  21.6 0.0 copy-start
  21.6 3.2 %copy-done = bf16[1024,4096]{1,0:T(8,128)(2,1)} copy-done((bf16[1024,4096]{1,0:T(8,128)(2,1)}, bf16[1024,4096]{1,0:T(8,128)(2,1)S(1)}, u32[]{:S(2)}) %copy-start) | copy-done | bytes 8388632
  24.8 212.0 %propagate.1 = (f32[1024,256]{1,0:T(8,128)}, f32[128,256]{1,0:T(8,128)}) custom-call(bf16[1024,256]{1,0:T(8,128)(2,1)} %bitcast.60, bf16[128,256]{1,0:T(8,128)(2,1)} %bitcast.62, f32[1024,256]{1,0:T(8,128)} %broadcast_in_dim.16.ru, f32[128,256]{1,0:T(8,128)} %broadcast_in_dim.17.ri, s32[256,128]{1,0:T(8,128)} %broadcast_in_dim.19.tu_col, ...), custom_call_target="tpu_custom_call" | custom-call | tf_op jit(solution)/shard_map/propagate/pallas_call | solution.py:515
  236.9 2.3 copy.16
  239.1 1.6 copy.17
Async XLA Ops:
  10.9 2.2 copy-start.1
  13.1 0.7 copy-start.2
  21.6 3.2 %copy-start = (bf16[1024,4096]{1,0:T(8,128)(2,1)}, bf16[1024,4096]{1,0:T(8,128)(2,1)S(1)}, u32[]{:S(2)}) copy-start(bf16[1024,4096]{1,0:T(8,128)(2,1)S(1)} %get-tuple-element.6.r_hbm) | copy-start | bytes 25165828

commit v2 on v0

v2 whole, which is shorter than its diff:
```python
import jax
import jax.numpy as jnp
from jax import lax
from jax.experimental import pallas as pl
from jax.experimental.pallas import tpu as pltpu
from jax.sharding import PartitionSpec as P

F32 = jnp.float32
BF16 = jnp.bfloat16
MESH = pl.DeviceIdType.MESH
SIDE = 4
BLOCK = 128
CHUNK = SIDE * BLOCK
HALF = SIDE * CHUNK
ROUNDS = 5
GROUPS = 8


def place(block):
    core = block & 1
    x = (block >> 1) & (SIDE - 1)
    y = block >> 3
    return core * SIDE * SIDE + (y + core * (x - y)) * SIDE + x + core * (y - x)


def build_kernel(count_ref, rows_ref, cols_ref, tiles_hbm, r_ref, tiles, sems):
    slots = tiles.shape[0]
    size = slots // GROUPS
    copies = [
        pltpu.make_async_copy(
            tiles_hbm.at[pl.ds(g * size, size)], tiles.at[pl.ds(g * size, size)], sems.at[g]
        )
        for g in range(GROUPS)
    ]
    for item in copies:
        item.start()
    step = 64

    def clear(i, carry):
        at = pl.ds(pl.multiple_of(i * step, step), step)
        for half in range(2):
            r_ref[half, at, :] = jnp.zeros((step, r_ref.shape[2]), BF16)
        return carry

    lax.fori_loop(0, r_ref.shape[1] // step, clear, 0)

    def add(slot, carry):
        spot = place(cols_ref[slot])
        half = spot // (SIDE * SIDE)
        users = pl.ds(pl.multiple_of(rows_ref[slot] * BLOCK, BLOCK), BLOCK)
        items = pl.ds(pl.multiple_of((spot % (SIDE * SIDE)) * BLOCK, BLOCK), BLOCK)
        tile = tiles[slot].astype(F32)
        r_ref[half, users, items] = (r_ref[half, users, items].astype(F32) + tile).astype(BF16)
        return carry

    count = count_ref[0]
    for g in range(GROUPS):
        copies[g].wait()
        lax.fori_loop(g * size, jnp.clip(count, g * size, (g + 1) * size), add, 0)


def build(count, rows, cols, tiles, users):
    smem = pl.BlockSpec(memory_space=pltpu.SMEM)
    return pl.pallas_call(
        build_kernel,
        out_shape=jax.ShapeDtypeStruct((2, users, HALF), BF16),
        in_specs=[smem, smem, smem, pl.BlockSpec(memory_space=pl.ANY)],
        out_specs=pl.BlockSpec(memory_space=pltpu.VMEM),
        scratch_shapes=[pltpu.VMEM(tiles.shape, jnp.int32), pltpu.SemaphoreType.DMA((GROUPS,))],
        compiler_params=pltpu.CompilerParams(vmem_limit_bytes=16 * 2**20),
        name="build",
    )(count, rows, cols, tiles)


def over_rows(left, right):
    return lax.dot_general(left, right, (((0,), (0,)), ((), ())), preferred_element_type=F32)


def main_kernel(
    user_emb, item_emb, user_degree, item_degree, triple_user, triple_pos, triple_neg, r_mat,
    out_user, out_item,
    feeds, users, sib_in, sib_out, q_out, q_in, p_out, p_in, z_out, z_in,
    part, upart, user_total, item_total, user_base, item_base, pick_u, pick_i, split, ru, ri,
    ag_recv, ag_send, rs_recv, rs_send, z_recv, z_send,
):
    a = lax.axis_index("user")
    z = lax.axis_index("item")
    core = a % 2
    x = (a // 2) % SIDE
    y = a // (2 * SIDE)
    p = x + core * (y - x)
    q = y + core * (x - y)
    rows_u = user_emb.shape[0]
    quarter = rows_u // SIDE
    trips = triple_user.shape[1]

    def at_pq(pp, qq):
        yy = qq + core * (pp - qq)
        xx = pp + core * (qq - pp)
        return {"user": (yy * SIDE + xx) * 2 + core}

    def turn(i, by):
        return (i + by) % SIDE

    to_p = {by: at_pq(turn(p, by), q) for by in (1, 2, 3)}
    to_q = {by: at_pq(p, turn(q, by)) for by in (1, 2, 3)}
    to_z = {by: {"item": turn(z, by)} for by in (1, 2, 3)}
    to_s = {"user": a + 1 - 2 * core}

    def rows(start, count):
        return pl.ds(pl.multiple_of(start, BLOCK), count)

    def copy(src, dst, send, recv, device):
        return pltpu.make_async_remote_copy(
            src_ref=src, dst_ref=dst, send_sem=send, recv_sem=recv,
            device_id=device, device_id_type=MESH,
        )

    barrier = pltpu.get_barrier_semaphore()
    partners = [*to_p.values(), *to_q.values(), *to_z.values(), to_s]
    for device in partners:
        pl.semaphore_signal(barrier, inc=1, device_id=device, device_id_type=MESH)

    def slot(qq, pp):
        return ((core * SIDE + qq) * SIDE + pp) * BLOCK

    def gather_copy(r, start, count, device, recv):
        ref = feeds.at[r, rows(start, count)]
        return copy(ref, ref, ag_send.at[r], ag_recv.at[r, recv], device)

    def to_sibling(r, qq, pp):
        gather_copy(r, slot(qq, pp), BLOCK, to_s, 15 + qq).start()

    def spread_block(r, rel):
        pp = turn(p, rel)
        for by in (2, 1, 3):
            gather_copy(r, slot(q, pp), BLOCK, to_q[by], 3 + (by - 1) * SIDE + rel).start()
        to_sibling(r, q, pp)

    def gather_start(r):
        for by in (2, 1, 3):
            gather_copy(r, slot(q, p), BLOCK, to_p[by], by - 1).start()
        spread_block(r, 0)

    def gather_p(r):
        for by in (1, 3, 2):
            back = turn(p, SIDE - by)
            gather_copy(r, slot(q, back), BLOCK, to_p[by], by - 1).wait_recv()
            spread_block(r, SIDE - by)

    def gather_q(r):
        for rel in (0, 3, 1, 2):
            pp = turn(p, rel)
            for by in (1, 3, 2):
                qq = turn(q, SIDE - by)
                gather_copy(
                    r, slot(qq, pp), BLOCK, to_q[by], 3 + (by - 1) * SIDE + rel
                ).wait_recv()
                to_sibling(r, qq, pp)

    def gather_end(r):
        for other in range(SIDE):
            start = ((1 - core) * SIDE + other) * CHUNK
            gather_copy(r, start, CHUNK, to_s, 15 + other).wait_recv()

    def gather_sent(r):
        gather_copy(r, 0, 31 * BLOCK, to_s, 0).wait_send()

    def feed_half(r, half):
        return feeds[r, rows(half * HALF, HALF), :]

    def sibling_part(r, term, rel):
        theirs = turn(p, rel)
        sib_out[theirs] = term(1 - core, theirs).astype(BF16)
        sibling_copy(r, theirs).start()

    def sibling_copy(r, chunk):
        return copy(
            sib_out.at[chunk], sib_in.at[r, chunk], rs_send.at[r, 0], rs_recv.at[r, chunk], to_s
        )

    def q_copy(r, by, rel):
        at = rows(turn(p, rel) * BLOCK, BLOCK)
        return copy(
            q_out.at[by - 1, at], q_in.at[r, by - 1, at], rs_send.at[r, 1],
            rs_recv.at[r, 4 + (by - 1) * SIDE + rel], to_q[by],
        )

    def p_copy(r, by):
        return copy(
            p_out.at[by - 1], p_in.at[r, by - 1], rs_send.at[r, 2],
            rs_recv.at[r, 15 + by], to_p[by],
        )

    def own_part(r, term, by):
        chunk = turn(q, by)
        part[...] = term(core, chunk)
        sibling_copy(r, chunk).wait_recv()
        value = part[...] + sib_in[r, chunk].astype(F32)
        if by == 0:
            part[...] = value
        else:
            q_out[by - 1] = value.astype(BF16)

    def q_send(r, bys, rels):
        for rel in rels:
            for by in bys:
                q_copy(r, by, rel).start()

    def sum_make(r, term, hook=None):
        if hook is None:
            for by in (2, 1, 3):
                sibling_part(r, term, by)
                own_part(r, term, by)
                q_send(r, (by,), (2, 1))
            q_send(r, (2, 1, 3), (3, 0))
            sibling_part(r, term, 0)
        else:
            for by in (2, 1, 3, 0):
                sibling_part(r, term, by)
            for by in (2, 1, 3):
                own_part(r, term, by)
            hook()
            q_send(r, (2, 1, 3), (2, 1, 3, 0))
        own_part(r, term, 0)

    def sum_q(r, rel):
        at = rows(turn(p, rel) * BLOCK, BLOCK)
        value = part[at, :]
        for by in (1, 3, 2):
            q_copy(r, by, rel).wait_recv()
            value = value + q_in[r, by - 1, at, :].astype(F32)
        return value

    def sum_p(r):
        for by in (2, 1, 3):
            p_out[by - 1] = sum_q(r, by).astype(BF16)
            p_copy(r, by).start()

    def sum_end(r):
        value = sum_q(r, 0)
        for by in (1, 3, 2):
            p_copy(r, by).wait_recv()
            value = value + p_in[r, by - 1].astype(F32)
        return value

    def sums_sent(r):
        copy(sib_out, sib_in.at[r], rs_send.at[r, 0], rs_recv.at[r, 0], to_s).wait_send()
        copy(q_out, q_in.at[r], rs_send.at[r, 1], rs_recv.at[r, 4], to_q[1]).wait_send()
        copy(p_out, p_in.at[r], rs_send.at[r, 2], rs_recv.at[r, 16], to_p[1]).wait_send()

    def z_copy(r, by):
        return copy(
            z_out.at[by - 1], z_in.at[r, by - 1], z_send.at[r, 0], z_recv.at[r, by - 1], to_z[by]
        )

    def u_copy(r, owner, by):
        ref = users.at[r + 1, rows(owner * quarter, quarter)]
        return copy(ref, ref, z_send.at[r, 1], z_recv.at[r, 2 + by], to_z[by])

    def users_make(r, term):
        for by in (2, 1, 3, 0):
            value = term(turn(z, by))
            if by == 0:
                upart[rows(z * quarter, quarter), :] = value
            else:
                z_out[by - 1] = value.astype(BF16)
                z_copy(r, by).start()

    def user_end(r):
        value = upart[rows(z * quarter, quarter), :]
        for by in (1, 3, 2):
            z_copy(r, by).wait_recv()
            value = value + z_in[r, by - 1].astype(F32)
        return value

    def user_spread(r, value):
        users[r + 1, rows(z * quarter, quarter), :] = value
        for by in (2, 1, 3):
            u_copy(r, z, by).start()

    def user_ready(r):
        for by in (1, 3, 2):
            u_copy(r, turn(z, SIDE - by), by).wait_recv()

    def users_sent(r):
        copy(z_out, z_in.at[r], z_send.at[r, 0], z_recv.at[r, 0], to_z[1]).wait_send()
        ref = users.at[r + 1, pl.ds(0, 3 * quarter)]
        copy(ref, ref, z_send.at[r, 1], z_recv.at[r, 3], to_z[1]).wait_send()

    def item_term(r):
        def term(half, chunk):
            return over_rows(r_mat[half, :, rows(chunk * CHUNK, CHUNK)], users[r])

        return term

    def users_first(r):
        def step(i, carry):
            at = rows(i * CHUNK, CHUNK)
            upart[at, :] = jnp.dot(
                r_mat[core, at, :], feed_half(r, core), preferred_element_type=F32
            )
            return carry

        lax.fori_loop(0, rows_u // CHUNK, step, 0)

    def user_term(r):
        def term(owner):
            at = rows(owner * quarter, quarter)
            return upart[at, :] + jnp.dot(
                r_mat[1 - core, at, :], feed_half(r, 1 - core), preferred_element_type=F32
            )

        return term

    def column(line):
        return jnp.broadcast_to(line, (BLOCK, BLOCK)).T

    def wide(scale):
        return jnp.concatenate([scale, scale], axis=1)

    own_u = rows(z * quarter, quarter)
    own_slot = rows(slot(q, p), BLOCK)

    def ru_own():
        return wide(ru[own_u, :])

    def ri_own():
        return wide(ri[...])

    ri[...] = column(lax.rsqrt(item_degree[...].astype(F32)))
    ei = item_emb[...].astype(F32)
    feeds[0, own_slot, :] = (ri_own() * ei).astype(BF16)
    pl.semaphore_wait(barrier, len(partners))
    gather_start(0)
    item_total[...] = ei
    for i in range(rows_u // BLOCK):
        at = slice(i * BLOCK, (i + 1) * BLOCK)
        scale = column(lax.rsqrt(user_degree[:, at].astype(F32)))
        ru[at, :] = scale
        users[0, at, :] = (wide(scale) * user_emb[at, :].astype(F32)).astype(BF16)
    user_total[...] = user_emb[own_u, :].astype(F32)

    def make_picks():
        def spot(ref):
            value = ref[...]
            return place(value >> 7) * BLOCK + (value & (BLOCK - 1))

        def columns(line):
            line = line.astype(F32)
            return jnp.concatenate(
                [column(line[:, i : i + BLOCK]) for i in range(0, trips, BLOCK)], axis=0
            )

        lane = lax.broadcasted_iota(jnp.int32, (trips, BLOCK), 1).astype(F32)
        chosen = columns(triple_user[...])
        for i in range(rows_u // BLOCK):
            hot = (chosen - i * BLOCK == lane).astype(F32)
            pick_u[:, i * BLOCK : (i + 1) * BLOCK] = hot.astype(BF16)
        pos = columns(spot(triple_pos))
        neg = columns(spot(triple_neg))
        for half in range(2):
            for i in range(HALF // BLOCK):
                at = half * HALF + i * BLOCK
                hot = (pos - at == lane).astype(F32) - (neg - at == lane).astype(F32)
                pick_i[half, :, i * BLOCK : (i + 1) * BLOCK] = hot.astype(BF16)

    def two_rounds(r, user_update, item_update, between):
        sum_make(r, item_term(r), lambda: gather_p(r))
        gather_q(r)
        users_first(r)
        gather_end(r)
        users_make(r, user_term(r))
        sum_p(r)
        item_update(r, sum_end(r))
        gather_start(r + 1)
        gather_p(r + 1)
        user_spread(r, user_update(r, user_end(r)))
        users_sent(r)
        sums_sent(r)
        between()
        gather_q(r + 1)
        users_first(r + 1)
        gather_end(r + 1)
        users_make(r + 1, user_term(r + 1))
        user_ready(r)
        sum_make(r + 1, item_term(r + 1))
        user_spread(r + 1, user_update(r + 1, user_end(r + 1)))
        sum_p(r + 1)
        item_update(r + 1, sum_end(r + 1))

    def forward_user(r, value):
        state = (ru_own() * value).astype(BF16).astype(F32)
        user_total[...] += state
        feed = ru_own() * state if r == 0 else user_total[...] / 3.0
        return feed.astype(BF16)

    def forward_item(r, value):
        state = (ri_own() * value).astype(BF16).astype(F32)
        item_total[...] += state
        feed = ri_own() * state if r == 0 else item_total[...] / 3.0
        feeds[r + 1, own_slot, :] = feed.astype(BF16)

    two_rounds(0, forward_user, forward_item, make_picks)

    gather_start(2)
    users_sent(1)
    sums_sent(1)
    gather_p(2)
    user_ready(1)
    user_rows = jnp.dot(pick_u[...], users[2], preferred_element_type=F32)
    upart[:trips, :] = user_rows
    gather_q(2)
    upart[trips : 2 * trips, :] = jnp.dot(
        pick_i[core], feed_half(2, core), preferred_element_type=F32
    )
    gather_end(2)
    diff = upart[trips : 2 * trips, :] + jnp.dot(
        pick_i[1 - core], feed_half(2, 1 - core), preferred_element_type=F32
    )
    user_rows = upart[:trips, :]
    score = jnp.sum(user_rows * diff, axis=1, keepdims=True)
    weight = -jax.nn.sigmoid(-score)
    for i, value in enumerate((weight * diff, weight * user_rows)):
        high = value.astype(BF16)
        split[i, :, :256] = high
        split[i, :, 256:] = (value - high.astype(F32)).astype(BF16)

    def both(product):
        return product[:, :256] + product[:, 256:]

    def grad_user_term(owner):
        return both(over_rows(pick_u[:, rows(owner * quarter, quarter)], split[0]))

    def grad_item_term(half, chunk):
        return both(over_rows(pick_i[half, :, rows(chunk * CHUNK, CHUNK)], split[1]))

    users_make(2, grad_user_term)
    sum_make(2, grad_item_term)
    value = user_end(2)
    user_base[...] = value
    user_spread(2, (ru_own() * value).astype(BF16))
    sum_p(2)
    value = sum_end(2)
    item_base[...] = value
    feeds[3, own_slot, :] = (ri_own() * value).astype(BF16)
    gather_start(3)
    users_sent(2)
    sums_sent(2)
    user_ready(2)

    def backward_user(r, value):
        state = user_base[...] + ru_own() * value
        return (ru_own() * state if r == 3 else state / 3.0).astype(BF16)

    def backward_item(r, value):
        state = item_base[...] + ri_own() * value
        if r == 3:
            feeds[r + 1, own_slot, :] = (ri_own() * state).astype(BF16)
        else:
            out_item[...] = state / 3.0

    two_rounds(3, backward_user, backward_item, lambda: None)
    user_ready(4)
    out_user[...] = users[5]
    users_sent(4)
    sums_sent(4)
    for r in range(ROUNDS):
        gather_sent(r)


def main(user_emb, item_emb, user_degree, item_degree, triples, r_mat):
    rows_u, width = user_emb.shape
    col_rows = 2 * HALF
    quarter = rows_u // SIDE
    trips = triples[0].shape[1]
    vmem = pl.BlockSpec(memory_space=pltpu.VMEM)
    dma = pltpu.SemaphoreType.DMA
    scratch = [
        pltpu.VMEM((ROUNDS, col_rows, width), BF16),
        pltpu.VMEM((ROUNDS + 1, rows_u, width), BF16),
        pltpu.VMEM((ROUNDS, SIDE, CHUNK, width), BF16),
        pltpu.VMEM((SIDE, CHUNK, width), BF16),
        pltpu.VMEM((3, CHUNK, width), BF16),
        pltpu.VMEM((ROUNDS, 3, CHUNK, width), BF16),
        pltpu.VMEM((3, BLOCK, width), BF16),
        pltpu.VMEM((ROUNDS, 3, BLOCK, width), BF16),
        pltpu.VMEM((3, quarter, width), BF16),
        pltpu.VMEM((ROUNDS, 3, quarter, width), BF16),
        pltpu.VMEM((CHUNK, width), F32),
        pltpu.VMEM((rows_u, width), F32),
        pltpu.VMEM((quarter, width), F32),
        pltpu.VMEM((BLOCK, width), F32),
        pltpu.VMEM((quarter, width), F32),
        pltpu.VMEM((BLOCK, width), F32),
        pltpu.VMEM((trips, rows_u), BF16),
        pltpu.VMEM((2, trips, HALF), BF16),
        pltpu.VMEM((2, trips, 2 * width), BF16),
        pltpu.VMEM((rows_u, BLOCK), F32),
        pltpu.VMEM((BLOCK, BLOCK), F32),
        dma((ROUNDS, 19)),
        dma((ROUNDS,)),
        dma((ROUNDS, 19)),
        dma((ROUNDS, 3)),
        dma((ROUNDS, 6)),
        dma((ROUNDS, 2)),
    ]
    return pl.pallas_call(
        main_kernel,
        out_shape=(
            jax.ShapeDtypeStruct((rows_u, width), BF16),
            jax.ShapeDtypeStruct((BLOCK, width), F32),
        ),
        in_specs=[vmem] * 8,
        out_specs=(vmem, vmem),
        scratch_shapes=scratch,
        compiler_params=pltpu.CompilerParams(
            collective_id=0, has_side_effects=True, vmem_limit_bytes=44 * 2**20
        ),
        name="propagate",
    )(user_emb, item_emb, user_degree, item_degree, *triples, r_mat)


def finish_kernel(user, item, out_user, out_item):
    out_user[...] = user[...].astype(F32)
    out_item[...] = item[...]


def finish(user, item):
    vmem = pl.BlockSpec(memory_space=pltpu.VMEM)
    return pl.pallas_call(
        finish_kernel,
        out_shape=(
            jax.ShapeDtypeStruct(user.shape, F32),
            jax.ShapeDtypeStruct(item.shape, F32),
        ),
        in_specs=[vmem, vmem],
        out_specs=(vmem, vmem),
        name="finish",
    )(user, item)


def per_device(
    user_emb, item_emb, user_degree, item_degree, tiles, tile_user, tile_item, tile_count,
    triple_user, triple_pos, triple_neg,
):
    r_mat = build(tile_count[0], tile_user[0, 0], tile_item[0, 0], tiles[0, 0], user_emb.shape[1])
    grad_user, grad_item = finish(*main(
        user_emb[0], item_emb[0, 0], user_degree, item_degree[0],
        (triple_user[0], triple_pos[0], triple_neg[0]), r_mat,
    ))
    return grad_user[None], grad_item[None, None]


def solution(mesh):
    return jax.shard_map(
        per_device,
        mesh=mesh,
        in_specs=(
            P("user", None, None),
            P("user", "item", None, None),
            P("user", None),
            P("user", "item", None),
            P("user", "item", None, None, None),
            P("user", "item", None),
            P("user", "item", None),
            P("user", "item"),
            P("user", "item", None),
            P("user", "item", None),
            P("user", "item", None),
        ),
        out_specs=(P("user", None, None), P("user", "item", None, None)),
        check_vma=False,
    )
```

time: 1030 us -> 163 us (0.16)
  waiting for transfers between devices: 739 us -> 0 us
  other arithmetic: 168 us -> 0 us
  Pallas kernels: 0 us -> 156 us
  matrix products: 53.4 us -> 0 us
  local copies, waits for them, and re-layouts: 48.4 us -> 4.95 us
  between operations: 14.8 us -> 1.45 us
    reduce_scatter x5 -> x0, waiting for transfers between devices: 386 us -> none  [settle(): lax.psum_scatter(term(jnp.int32(0), lax.axis_size('user') * rows_i), 'use...]
    all_gather x5 -> x0, waiting for transfers between devices: 200 us -> none  [spread(): return lax.all_gather(feed, 'user', axis=0, tiled=True)]
    pallas_call x0 -> x3, Pallas kernels: none -> 156 us  [the longest x1 152 us: main(): pl.pallas_call(main_kernel, out_shape=(jax.ShapeDtypeStruct((rows_u, widt...]
    psum x3 -> x0, waiting for transfers between devices: 152 us -> none  [total_users(): return lax.psum(part, 'item')]
    scatter-add x11 -> x0, other arithmetic: 151 us -> none  [the longest x4 76 us: item_terms(): jax.ops.segment_sum(prods, tile_cols, num_segments=col_blocks)]
    dot_general x8 -> x0, matrix products: 53.4 us -> none  [the longest x4 26.8 us: item_terms(): jnp.einsum('tuv,tud->tvd', tile_mats, picked, preferred_element_type=jnp....]
    gather x11 -> x0, local copies, waits for them, and re-layouts: 35.4 us -> none  [the longest x4 17.4 us: user_side(): picked = feed_col.reshape(col_blocks, block, width)[tile_cols]]
    another operation x8 -> x0, local copies, waits for them, and re-layouts: 12.4 us -> none
  transfers between devices with their start and end apart: 13 -> 0, of which waited for: 13 -> 0; matrix products, arithmetic and copies ran while one was open for 6% -> 0% of each run, Pallas kernels for 0% -> 0%
where the time goes in v2:
time: 163 us; the launch traced here: 162 us
  Pallas kernels  156 us (96%)
  local copies, waits for them, and re-layouts  4.95 us (3%)
    pallas_call x1, Pallas kernels, main(): pl.pallas_call(main_kernel, out_shape=(jax.ShapeDtypeStruct((rows_u, widt...  152 us
    unnamed x24, local copies, waits for them, and re-layouts  4.95 us

profile of v2, /device:TPU:0, one launch (start us, length us, event | category | flops | bytes accessed | tf_op | source)
XLA Modules:
  0.0 162.2 jit_solution(2396245308570190729)
XLA Ops:
  0.6 0.0 copy-start.8
  0.6 0.0 copy-start.7
  0.7 0.0 copy-start.6
  0.7 0.0 copy-start.11
  0.7 0.0 copy-start.5
  1.4 0.0 copy-start
  1.4 2.2 %copy-done = s32[1,1,64,128,128]{4,3,2,1,0:T(8,128)S(1)} copy-done((s32[1,1,64,128,128]{4,3,2,1,0:T(8,128)S(1)}, s32[1,1,64,128,128]{4,3,2,1,0:T(8,128)}, u32[]{:S(2)}) %copy-start) | copy-done | bytes 4194328
  3.6 0.7 copy-done.9
  4.2 0.0 copy-start.10
  4.2 0.7 copy-done.10
  4.9 0.0 copy-start.1
  4.9 1.8 %build.1.r_mat = bf16[2,1024,2048]{2,1,0:T(8,128)(2,1)S(1)} custom-call(s32[1]{0:T(128)} %bitcast.12.count_ref, s32[64]{0:T(128)S(1)} %bitcast.19, s32[64]{0:T(128)S(1)} %bitcast.20, s32[64,128,128]{2,1,0:T(8,128)S(1)} %bitcast.13), custom_call_target="tpu_custom_call" | custom-call | tf_op jit(solution)/shard_map/build/pallas_call | solution.py:64
  6.7 0.0 copy-done.8
  6.7 0.0 copy-done.7
  6.7 0.0 copy-done.6
  6.7 0.0 copy-done.11
  6.7 0.0 copy-done.5
  6.7 0.0 copy-done.1
  6.7 0.0 copy-done.4
  6.7 151.9 %propagate.1 = (bf16[1024,256]{1,0:T(8,128)(2,1)S(1)}, f32[128,256]{1,0:T(8,128)S(1)}) custom-call(bf16[1024,256]{1,0:T(8,128)(2,1)S(1)} %bitcast.14, bf16[128,256]{1,0:T(8,128)(2,1)S(1)} %bitcast.15, s32[1,1024]{1,0:T(1,128)S(1)} %copy-done.5, s32[1,128]{1,0:T(1,128)S(1)} %bitcast.21, s32[1,256]{1,0:T(1,128)S(1)} %bitcast.16, s32[1,256]{1,0:T(1,128)S(1)} %bitcast.17, ...), custom_call_target="tpu_custom_call" | custom-call | tf_op jit(solution)/shard_map/propagate/pallas_call | solution.py:508
  158.6 0.0 copy-start.2
  158.6 0.8 copy-done.2
  159.4 0.6 copy-done.3
  160.1 2.1 %finish.1 = (f32[1024,256]{1,0:T(8,128)}, f32[128,256]{1,0:T(8,128)}) custom-call(bf16[1024,256]{1,0:T(8,128)(2,1)} %copy-done.2, f32[128,256]{1,0:T(8,128)} %copy-done.3), custom_call_target="tpu_custom_call" | custom-call | tf_op jit(solution)/shard_map/finish/pallas_call | solution.py:531
  (3 shorter events, 0.0 us)
Async XLA Ops:
  0.6 6.0 %copy-start.8 = (s32[1,1,256]{2,1,0:T(1,128)S(1)}, s32[1,1,256]{2,1,0:T(1,128)}, u32[]{:S(2)}) copy-start(s32[1,1,256]{2,1,0:T(1,128)} %param.21) | copy-start | bytes 3076
  0.6 6.0 %copy-start.7 = (s32[1,1,256]{2,1,0:T(1,128)S(1)}, s32[1,1,256]{2,1,0:T(1,128)}, u32[]{:S(2)}) copy-start(s32[1,1,256]{2,1,0:T(1,128)} %param.20) | copy-start | bytes 3076
  0.7 6.0 %copy-start.6 = (s32[1,1,256]{2,1,0:T(1,128)S(1)}, s32[1,1,256]{2,1,0:T(1,128)}, u32[]{:S(2)}) copy-start(s32[1,1,256]{2,1,0:T(1,128)} %param.19) | copy-start | bytes 3076
  0.7 6.0 %copy-start.11 = (s32[1,1,128]{2,1,0:T(1,128)S(1)}, s32[1,1,128]{2,1,0:T(1,128)}, u32[]{:S(2)}) copy-start(s32[1,1,128]{2,1,0:T(1,128)} %param.14) | copy-start | bytes 1540
  0.7 6.0 %copy-start.5 = (s32[1,1024]{1,0:T(1,128)S(1)}, s32[1,1024]{1,0:T(1,128)}, u32[]{:S(2)}) copy-start(s32[1,1024]{1,0:T(1,128)} %user_degree.1) | copy-start | bytes 12292
  1.4 2.2 %copy-start = (s32[1,1,64,128,128]{4,3,2,1,0:T(8,128)S(1)}, s32[1,1,64,128,128]{4,3,2,1,0:T(8,128)}, u32[]{:S(2)}) copy-start(s32[1,1,64,128,128]{4,3,2,1,0:T(8,128)} %param.15) | copy-start | bytes 12582916
  3.6 0.7 copy-start.9
  4.2 0.7 copy-start.10
  4.9 1.8 %copy-start.1 = (bf16[1,1024,256]{2,1,0:T(8,128)(2,1)S(1)}, bf16[1,1024,256]{2,1,0:T(8,128)(2,1)}, u32[]{:S(2)}) copy-start(bf16[1,1024,256]{2,1,0:T(8,128)(2,1)} %param.11) | copy-start | bytes 1572868
  4.9 1.8 %copy-start.4 = (bf16[1,1,128,256]{3,2,1,0:T(8,128)(2,1)S(1)}, bf16[1,1,128,256]{3,2,1,0:T(8,128)(2,1)}, u32[]{:S(2)}) copy-start(bf16[1,1,128,256]{3,2,1,0:T(8,128)(2,1)} %param.12) | copy-start | bytes 196612
  158.6 0.8 copy-start.2
  159.4 0.6 copy-start.3

commit v3 on v2

--- a/solution.py
+++ b/solution.py
@@ -23,8 +23,18 @@
     return core * SIDE * SIDE + (y + core * (x - y)) * SIDE + x + core * (y - x)
 
 
-def build_kernel(count_ref, rows_ref, cols_ref, tiles_hbm, r_ref, tiles, sems):
+def build_kernel(
+    count_hbm, rows_hbm, cols_hbm, tiles_hbm, r_ref, count_ref, rows_ref, cols_ref, tiles, sems
+):
     slots = tiles.shape[0]
+    scalars = [
+        pltpu.make_async_copy(src, dst, sems.at[GROUPS + i])
+        for i, (src, dst) in enumerate(
+            ((count_hbm, count_ref), (rows_hbm, rows_ref), (cols_hbm, cols_ref))
+        )
+    ]
+    for item in scalars:
+        item.start()
     size = slots // GROUPS
     copies = [
         pltpu.make_async_copy(
@@ -45,28 +55,36 @@
     lax.fori_loop(0, r_ref.shape[1] // step, clear, 0)
 
     def add(slot, carry):
-        spot = place(cols_ref[slot])
+        spot = place(cols_ref[0, slot])
         half = spot // (SIDE * SIDE)
-        users = pl.ds(pl.multiple_of(rows_ref[slot] * BLOCK, BLOCK), BLOCK)
+        users = pl.ds(pl.multiple_of(rows_ref[0, slot] * BLOCK, BLOCK), BLOCK)
         items = pl.ds(pl.multiple_of((spot % (SIDE * SIDE)) * BLOCK, BLOCK), BLOCK)
         tile = tiles[slot].astype(F32)
         r_ref[half, users, items] = (r_ref[half, users, items].astype(F32) + tile).astype(BF16)
         return carry
 
-    count = count_ref[0]
+    for item in scalars:
+        item.wait()
+    count = count_ref[0, 0]
     for g in range(GROUPS):
         copies[g].wait()
         lax.fori_loop(g * size, jnp.clip(count, g * size, (g + 1) * size), add, 0)
 
 
 def build(count, rows, cols, tiles, users):
-    smem = pl.BlockSpec(memory_space=pltpu.SMEM)
+    hbm = pl.BlockSpec(memory_space=pl.ANY)
     return pl.pallas_call(
         build_kernel,
         out_shape=jax.ShapeDtypeStruct((2, users, HALF), BF16),
-        in_specs=[smem, smem, smem, pl.BlockSpec(memory_space=pl.ANY)],
+        in_specs=[hbm] * 4,
         out_specs=pl.BlockSpec(memory_space=pltpu.VMEM),
-        scratch_shapes=[pltpu.VMEM(tiles.shape, jnp.int32), pltpu.SemaphoreType.DMA((GROUPS,))],
+        scratch_shapes=[
+            pltpu.SMEM(count.shape, jnp.int32),
+            pltpu.SMEM(rows.shape, jnp.int32),
+            pltpu.SMEM(cols.shape, jnp.int32),
+            pltpu.VMEM(tiles.shape, jnp.int32),
+            pltpu.SemaphoreType.DMA((GROUPS + 3,)),
+        ],
         compiler_params=pltpu.CompilerParams(vmem_limit_bytes=16 * 2**20),
         name="build",
     )(count, rows, cols, tiles)
@@ -77,11 +95,13 @@
 
 
 def main_kernel(
-    user_emb, item_emb, user_degree, item_degree, triple_user, triple_pos, triple_neg, r_mat,
+    user_emb_hbm, item_emb_hbm, user_degree_hbm, item_degree_hbm, triple_user_hbm,
+    triple_pos_hbm, triple_neg_hbm, r_mat,
     out_user, out_item,
+    user_emb, item_emb, user_degree, item_degree, triple_user, triple_pos, triple_neg,
     feeds, users, sib_in, sib_out, q_out, q_in, p_out, p_in, z_out, z_in,
     part, upart, user_total, item_total, user_base, item_base, pick_u, pick_i, split, ru, ri,
-    ag_recv, ag_send, rs_recv, rs_send, z_recv, z_send,
+    load_sem, ag_recv, ag_send, rs_recv, rs_send, z_recv, z_send,
 ):
     a = lax.axis_index("user")
     z = lax.axis_index("item")
@@ -93,6 +113,7 @@
     rows_u = user_emb.shape[0]
     quarter = rows_u // SIDE
     trips = triple_user.shape[1]
+    half_q = quarter // 2
 
     def at_pq(pp, qq):
         yy = qq + core * (pp - qq)
@@ -116,6 +137,17 @@
             device_id=device, device_id_type=MESH,
         )
 
+    loads = [
+        pltpu.make_async_copy(src, dst, load_sem.at[i])
+        for i, (src, dst) in enumerate((
+            (item_degree_hbm, item_degree), (item_emb_hbm, item_emb),
+            (user_degree_hbm, user_degree), (user_emb_hbm, user_emb),
+            (triple_user_hbm, triple_user), (triple_pos_hbm, triple_pos),
+            (triple_neg_hbm, triple_neg),
+        ))
+    ]
+    for load in loads:
+        load.start()
     barrier = pltpu.get_barrier_semaphore()
     partners = [*to_p.values(), *to_q.values(), *to_z.values(), to_s]
     for device in partners:
@@ -148,8 +180,10 @@
             gather_copy(r, slot(q, back), BLOCK, to_p[by], by - 1).wait_recv()
             spread_block(r, SIDE - by)
 
-    def gather_q(r):
+    def gather_q(r, hook=None):
         for rel in (0, 3, 1, 2):
+            if rel == 1 and hook is not None:
+                hook()
             pp = turn(p, rel)
             for by in (1, 3, 2):
                 qq = turn(q, SIDE - by)
@@ -207,21 +241,13 @@
             for by in bys:
                 q_copy(r, by, rel).start()
 
-    def sum_make(r, term, hook=None):
-        if hook is None:
-            for by in (2, 1, 3):
-                sibling_part(r, term, by)
-                own_part(r, term, by)
-                q_send(r, (by,), (2, 1))
-            q_send(r, (2, 1, 3), (3, 0))
-            sibling_part(r, term, 0)
-        else:
-            for by in (2, 1, 3, 0):
-                sibling_part(r, term, by)
-            for by in (2, 1, 3):
-                own_part(r, term, by)
-            hook()
-            q_send(r, (2, 1, 3), (2, 1, 3, 0))
+    def sum_make(r, term):
+        sibling_part(r, term, 2)
+        for by, later in ((2, 1), (1, 3), (3, 0)):
+            sibling_part(r, term, later)
+            own_part(r, term, by)
+            q_send(r, (by,), (2, 1))
+        q_send(r, (2, 1, 3), (3, 0))
         own_part(r, term, 0)
 
     def sum_q(r, rel):
@@ -249,44 +275,47 @@
         copy(q_out, q_in.at[r], rs_send.at[r, 1], rs_recv.at[r, 4], to_q[1]).wait_send()
         copy(p_out, p_in.at[r], rs_send.at[r, 2], rs_recv.at[r, 16], to_p[1]).wait_send()
 
-    def z_copy(r, by):
+    def z_copy(r, by, sub):
+        at = rows(sub * half_q, half_q)
         return copy(
-            z_out.at[by - 1], z_in.at[r, by - 1], z_send.at[r, 0], z_recv.at[r, by - 1], to_z[by]
+            z_out.at[by - 1, at], z_in.at[r, by - 1, at], z_send.at[r, 0],
+            z_recv.at[r, (by - 1) * 2 + sub], to_z[by],
         )
 
-    def u_copy(r, owner, by):
-        ref = users.at[r + 1, rows(owner * quarter, quarter)]
-        return copy(ref, ref, z_send.at[r, 1], z_recv.at[r, 2 + by], to_z[by])
+    def u_copy(r, owner, by, sub):
+        ref = users.at[r + 1, rows(owner * quarter + sub * half_q, half_q)]
+        return copy(ref, ref, z_send.at[r, 1], z_recv.at[r, 4 + by * 2 + sub], to_z[by])
 
     def users_make(r, term):
-        for by in (2, 1, 3, 0):
-            value = term(turn(z, by))
-            if by == 0:
-                upart[rows(z * quarter, quarter), :] = value
-            else:
-                z_out[by - 1] = value.astype(BF16)
-                z_copy(r, by).start()
-
-    def user_end(r):
-        value = upart[rows(z * quarter, quarter), :]
+        for by in (2, 1, 3):
+            z_out[by - 1] = term(turn(z, by)).astype(BF16)
+            z_copy(r, by, 0).start()
+        for by in (2, 1, 3):
+            z_copy(r, by, 1).start()
+        upart[rows(z * quarter, quarter), :] = term(z)
+
+    def user_turn(r, sub, update):
+        at = rows(z * quarter + sub * half_q, half_q)
+        own = slice(sub * half_q, (sub + 1) * half_q)
+        value = upart[at, :]
         for by in (1, 3, 2):
-            z_copy(r, by).wait_recv()
-            value = value + z_in[r, by - 1].astype(F32)
-        return value
-
-    def user_spread(r, value):
-        users[r + 1, rows(z * quarter, quarter), :] = value
+            z_copy(r, by, sub).wait_recv()
+            value = value + z_in[r, by - 1, own, :].astype(F32)
+        users[r + 1, at, :] = update(r, own, wide(ru[at, :]), value).astype(BF16)
         for by in (2, 1, 3):
-            u_copy(r, z, by).start()
+            u_copy(r, z, by, sub).start()
 
     def user_ready(r):
-        for by in (1, 3, 2):
-            u_copy(r, turn(z, SIDE - by), by).wait_recv()
-
-    def users_sent(r):
+        for sub in range(2):
+            for by in (1, 3, 2):
+                u_copy(r, turn(z, SIDE - by), by, sub).wait_recv()
+
+    def z_sent(r):
         copy(z_out, z_in.at[r], z_send.at[r, 0], z_recv.at[r, 0], to_z[1]).wait_send()
+
+    def u_sent(r):
         ref = users.at[r + 1, pl.ds(0, 3 * quarter)]
-        copy(ref, ref, z_send.at[r, 1], z_recv.at[r, 3], to_z[1]).wait_send()
+        copy(ref, ref, z_send.at[r, 1], z_recv.at[r, 6], to_z[1]).wait_send()
 
     def item_term(r):
         def term(half, chunk):
@@ -322,18 +351,19 @@
     own_u = rows(z * quarter, quarter)
     own_slot = rows(slot(q, p), BLOCK)
 
-    def ru_own():
-        return wide(ru[own_u, :])
-
     def ri_own():
         return wide(ri[...])
 
+    for load in loads[:2]:
+        load.wait()
     ri[...] = column(lax.rsqrt(item_degree[...].astype(F32)))
     ei = item_emb[...].astype(F32)
     feeds[0, own_slot, :] = (ri_own() * ei).astype(BF16)
     pl.semaphore_wait(barrier, len(partners))
     gather_start(0)
     item_total[...] = ei
+    for load in loads[2:]:
+        load.wait()
     for i in range(rows_u // BLOCK):
         at = slice(i * BLOCK, (i + 1) * BLOCK)
         scale = column(lax.rsqrt(user_degree[:, at].astype(F32)))
@@ -365,52 +395,54 @@
                 hot = (pos - at == lane).astype(F32) - (neg - at == lane).astype(F32)
                 pick_i[half, :, i * BLOCK : (i + 1) * BLOCK] = hot.astype(BF16)
 
-    def two_rounds(r, user_update, item_update, between):
-        sum_make(r, item_term(r), lambda: gather_p(r))
-        gather_q(r)
-        users_first(r)
+    def users_last(r):
         gather_end(r)
+        if r > 0:
+            z_sent(r - 1)
         users_make(r, user_term(r))
-        sum_p(r)
-        item_update(r, sum_end(r))
-        gather_start(r + 1)
-        gather_p(r + 1)
-        user_spread(r, user_update(r, user_end(r)))
-        users_sent(r)
-        sums_sent(r)
-        between()
-        gather_q(r + 1)
-        users_first(r + 1)
-        gather_end(r + 1)
-        users_make(r + 1, user_term(r + 1))
-        user_ready(r)
-        sum_make(r + 1, item_term(r + 1))
-        user_spread(r + 1, user_update(r + 1, user_end(r + 1)))
-        sum_p(r + 1)
-        item_update(r + 1, sum_end(r + 1))
-
-    def forward_user(r, value):
-        state = (ru_own() * value).astype(BF16).astype(F32)
-        user_total[...] += state
-        feed = ru_own() * state if r == 0 else user_total[...] / 3.0
-        return feed.astype(BF16)
+
+    def forward_user(r, own, scale, value):
+        state = (scale * value).astype(BF16).astype(F32)
+        user_total[own, :] += state
+        return scale * state if r == 0 else user_total[own, :] / 3.0
 
     def forward_item(r, value):
         state = (ri_own() * value).astype(BF16).astype(F32)
         item_total[...] += state
         feed = ri_own() * state if r == 0 else item_total[...] / 3.0
         feeds[r + 1, own_slot, :] = feed.astype(BF16)
-
-    two_rounds(0, forward_user, forward_item, make_picks)
-
-    gather_start(2)
-    users_sent(1)
-    sums_sent(1)
+        gather_start(r + 1)
+
+    term = item_term(0)
+    for by in (2, 1, 3, 0):
+        sibling_part(0, term, by)
+    gather_p(0)
+    for by in (2, 1, 3, 0):
+        own_part(0, term, by)
+    gather_q(0, lambda: q_send(0, (2, 1, 3), (2, 1, 3, 0)))
+    users_first(0)
+    users_last(0)
+    sum_p(0)
+    forward_item(0, sum_end(0))
+    user_turn(0, 0, forward_user)
+    user_turn(0, 1, forward_user)
+    make_picks()
+    gather_p(1)
+    sums_sent(0)
+    user_ready(0)
+    sum_make(1, item_term(1))
+    gather_q(1)
+    users_first(1)
+    sum_p(1)
+    users_last(1)
+    forward_item(1, sum_end(1))
+    user_turn(1, 0, forward_user)
+    user_turn(1, 1, forward_user)
+
     gather_p(2)
+    gather_q(2)
     user_ready(1)
-    user_rows = jnp.dot(pick_u[...], users[2], preferred_element_type=F32)
-    upart[:trips, :] = user_rows
-    gather_q(2)
+    upart[:trips, :] = jnp.dot(pick_u[...], users[2], preferred_element_type=F32)
     upart[trips : 2 * trips, :] = jnp.dot(
         pick_i[core], feed_half(2, core), preferred_element_type=F32
     )
@@ -435,37 +467,55 @@
     def grad_item_term(half, chunk):
         return both(over_rows(pick_i[half, :, rows(chunk * CHUNK, CHUNK)], split[1]))
 
+    def grad_user(r, own, scale, value):
+        user_base[own, :] = value
+        return scale * value
+
+    z_sent(1)
     users_make(2, grad_user_term)
+    sums_sent(1)
     sum_make(2, grad_item_term)
-    value = user_end(2)
-    user_base[...] = value
-    user_spread(2, (ru_own() * value).astype(BF16))
+    user_turn(2, 0, grad_user)
+    user_turn(2, 1, grad_user)
     sum_p(2)
     value = sum_end(2)
     item_base[...] = value
     feeds[3, own_slot, :] = (ri_own() * value).astype(BF16)
     gather_start(3)
-    users_sent(2)
+
+    def backward_user(r, own, scale, value):
+        state = user_base[own, :] + scale * value
+        return scale * state if r == 3 else state / 3.0
+
     sums_sent(2)
     user_ready(2)
-
-    def backward_user(r, value):
-        state = user_base[...] + ru_own() * value
-        return (ru_own() * state if r == 3 else state / 3.0).astype(BF16)
-
-    def backward_item(r, value):
-        state = item_base[...] + ri_own() * value
-        if r == 3:
-            feeds[r + 1, own_slot, :] = (ri_own() * state).astype(BF16)
-        else:
-            out_item[...] = state / 3.0
-
-    two_rounds(3, backward_user, backward_item, lambda: None)
+    sum_make(3, item_term(3))
+    gather_p(3)
+    gather_q(3, lambda: sum_p(3))
+    state = item_base[...] + ri_own() * sum_end(3)
+    feeds[4, own_slot, :] = (ri_own() * state).astype(BF16)
+    gather_start(4)
+    users_first(3)
+    users_last(3)
+    gather_p(4)
+    user_turn(3, 0, backward_user)
+    user_turn(3, 1, backward_user)
+    gather_q(4)
+    users_first(4)
+    users_last(4)
+    sums_sent(3)
+    user_ready(3)
+    sum_make(4, item_term(4))
+    user_turn(4, 0, backward_user)
+    user_turn(4, 1, backward_user)
+    sum_p(4)
+    out_item[...] = item_base[...] + ri_own() * sum_end(4)
     user_ready(4)
     out_user[...] = users[5]
-    users_sent(4)
     sums_sent(4)
+    z_sent(4)
     for r in range(ROUNDS):
+        u_sent(r)
         gather_sent(r)
 
 
@@ -476,7 +526,8 @@
     trips = triples[0].shape[1]
     vmem = pl.BlockSpec(memory_space=pltpu.VMEM)
     dma = pltpu.SemaphoreType.DMA
-    scratch = [
+    small = (user_emb, item_emb, user_degree, item_degree, *triples)
+    scratch = [pltpu.VMEM(v.shape, v.dtype) for v in small] + [
         pltpu.VMEM((ROUNDS, col_rows, width), BF16),
         pltpu.VMEM((ROUNDS + 1, rows_u, width), BF16),
         pltpu.VMEM((ROUNDS, SIDE, CHUNK, width), BF16),
@@ -498,11 +549,12 @@
         pltpu.VMEM((2, trips, 2 * width), BF16),
         pltpu.VMEM((rows_u, BLOCK), F32),
         pltpu.VMEM((BLOCK, BLOCK), F32),
+        dma((7,)),
         dma((ROUNDS, 19)),
         dma((ROUNDS,)),
         dma((ROUNDS, 19)),
         dma((ROUNDS, 3)),
-        dma((ROUNDS, 6)),
+        dma((ROUNDS, 12)),
         dma((ROUNDS, 2)),
     ]
     return pl.pallas_call(
@@ -511,45 +563,26 @@
             jax.ShapeDtypeStruct((rows_u, width), BF16),
             jax.ShapeDtypeStruct((BLOCK, width), F32),
         ),
-        in_specs=[vmem] * 8,
+        in_specs=[pl.BlockSpec(memory_space=pl.ANY)] * 7 + [vmem],
         out_specs=(vmem, vmem),
         scratch_shapes=scratch,
         compiler_params=pltpu.CompilerParams(
             collective_id=0, has_side_effects=True, vmem_limit_bytes=44 * 2**20
         ),
         name="propagate",
-    )(user_emb, item_emb, user_degree, item_degree, *triples, r_mat)
-
-
-def finish_kernel(user, item, out_user, out_item):
-    out_user[...] = user[...].astype(F32)
-    out_item[...] = item[...]
-
-
-def finish(user, item):
-    vmem = pl.BlockSpec(memory_space=pltpu.VMEM)
-    return pl.pallas_call(
-        finish_kernel,
-        out_shape=(
-            jax.ShapeDtypeStruct(user.shape, F32),
-            jax.ShapeDtypeStruct(item.shape, F32),
-        ),
-        in_specs=[vmem, vmem],
-        out_specs=(vmem, vmem),
-        name="finish",
-    )(user, item)
+    )(*small, r_mat)
 
 
 def per_device(
     user_emb, item_emb, user_degree, item_degree, tiles, tile_user, tile_item, tile_count,
     triple_user, triple_pos, triple_neg,
 ):
-    r_mat = build(tile_count[0], tile_user[0, 0], tile_item[0, 0], tiles[0, 0], user_emb.shape[1])
-    grad_user, grad_item = finish(*main(
+    r_mat = build(tile_count, tile_user[0], tile_item[0], tiles[0, 0], user_emb.shape[1])
+    grad_user, grad_item = main(
         user_emb[0], item_emb[0, 0], user_degree, item_degree[0],
         (triple_user[0], triple_pos[0], triple_neg[0]), r_mat,
-    ))
-    return grad_user[None], grad_item[None, None]
+    )
+    return grad_user.astype(F32)[None], (grad_item / 3.0)[None, None]
 
 
 def solution(mesh):

time: 163 us -> 146 us (0.90)
  Pallas kernels: 156 us -> 137 us
  other arithmetic: 0 us -> 1.71 us
    pallas_call x1, Pallas kernels: 152 us -> 135 us  [main(): pl.pallas_call(main_kernel, out_shape=(jax.ShapeDtypeStruct((rows_u, widt...]
    pallas_call x1 -> x0, Pallas kernels: 2.14 us -> none  [finish(): pl.pallas_call(finish_kernel, out_shape=(jax.ShapeDtypeStruct(user.shape,...]
    broadcast_in_dim x0 -> x2, other arithmetic: none -> 1.71 us  [per_device(): return (grad_user.astype(F32)[None], (grad_item / 3.0)[None, None])]
    unnamed x24 -> x20, local copies, waits for them, and re-layouts: 4.95 us -> 3.52 us
where the time goes in v3:
time: 146 us; the launch traced here: 144 us
  Pallas kernels  137 us (94%)
  local copies, waits for them, and re-layouts  3.52 us (2%)
  other arithmetic  1.71 us (1%)
    pallas_call x1, Pallas kernels, main(): pl.pallas_call(main_kernel, out_shape=(jax.ShapeDtypeStruct((rows_u, widt...  135 us
    unnamed x20, local copies, waits for them, and re-layouts  3.52 us

profile of v3, /device:TPU:0, one launch (start us, length us, event | category | flops | bytes accessed | tf_op | source)
XLA Modules:
  0.0 143.8 jit_solution(5578453669759117581)
XLA Ops:
  0.6 0.0 copy-start.6
  0.6 0.0 copy-start.5
  0.7 0.0 copy-start.4
  0.7 0.0 copy-start.9
  0.7 0.0 copy-start.3
  1.4 0.0 copy-start
  1.4 2.2 %copy-done = s32[1,1,64,128,128]{4,3,2,1,0:T(8,128)S(1)} copy-done((s32[1,1,64,128,128]{4,3,2,1,0:T(8,128)S(1)}, s32[1,1,64,128,128]{4,3,2,1,0:T(8,128)}, u32[]{:S(2)}) %copy-start) | copy-done | bytes 4194328
  3.6 0.0 copy-start.7
  3.6 0.7 copy-done.7
  4.2 0.0 copy-start.8
  4.2 0.7 copy-done.8
  4.9 0.0 copy-start.1
  4.9 0.0 copy-start.2
  4.9 1.7 %build.1.r_mat = bf16[2,1024,2048]{2,1,0:T(8,128)(2,1)S(1)} custom-call(s32[1,1]{1,0:T(1,128)S(6)} %copy.13.count_hbm, s32[1,64]{1,0:T(1,128)S(1)} %bitcast.20, s32[1,64]{1,0:T(1,128)S(1)} %bitcast.21, s32[64,128,128]{2,1,0:T(8,128)S(1)} %bitcast.14), custom_call_target="tpu_custom_call" | custom-call | tf_op jit(solution)/shard_map/build/pallas_call | solution.py:76
  6.6 0.0 copy-done.6
  6.6 0.0 copy-done.5
  6.6 0.0 copy-done.4
  6.6 0.0 copy-done.9
  6.6 0.0 copy-done.3
  6.6 0.0 copy-done.1
  6.6 0.0 copy-done.2
  6.7 135.4 %propagate.1 = (bf16[1024,256]{1,0:T(8,128)(2,1)S(1)}, f32[128,256]{1,0:T(8,128)S(1)}) custom-call(bf16[1024,256]{1,0:T(8,128)(2,1)S(1)} %bitcast.15, bf16[128,256]{1,0:T(8,128)(2,1)S(1)} %bitcast.16, s32[1,1024]{1,0:T(1,128)S(1)} %copy-done.3, s32[1,128]{1,0:T(1,128)S(1)} %bitcast.22, s32[1,256]{1,0:T(1,128)S(1)} %bitcast.17, s32[1,256]{1,0:T(1,128)S(1)} %bitcast.18, ...), custom_call_target="tpu_custom_call" | custom-call | tf_op jit(solution)/shard_map/propagate/pallas_call | solution.py:560
  142.1 0.7 multiply_bitcast_fusion
  142.8 1.0 bitcast_convert_fusion
Async XLA Ops:
  0.6 6.0 %copy-start.6 = (s32[1,1,256]{2,1,0:T(1,128)S(1)}, s32[1,1,256]{2,1,0:T(1,128)}, u32[]{:S(2)}) copy-start(s32[1,1,256]{2,1,0:T(1,128)} %param.21) | copy-start | bytes 3076
  0.6 6.0 %copy-start.5 = (s32[1,1,256]{2,1,0:T(1,128)S(1)}, s32[1,1,256]{2,1,0:T(1,128)}, u32[]{:S(2)}) copy-start(s32[1,1,256]{2,1,0:T(1,128)} %param.20) | copy-start | bytes 3076
  0.7 6.0 %copy-start.4 = (s32[1,1,256]{2,1,0:T(1,128)S(1)}, s32[1,1,256]{2,1,0:T(1,128)}, u32[]{:S(2)}) copy-start(s32[1,1,256]{2,1,0:T(1,128)} %param.19) | copy-start | bytes 3076
  0.7 6.0 %copy-start.9 = (s32[1,1,128]{2,1,0:T(1,128)S(1)}, s32[1,1,128]{2,1,0:T(1,128)}, u32[]{:S(2)}) copy-start(s32[1,1,128]{2,1,0:T(1,128)} %param.14) | copy-start | bytes 1540
  0.7 6.0 %copy-start.3 = (s32[1,1024]{1,0:T(1,128)S(1)}, s32[1,1024]{1,0:T(1,128)}, u32[]{:S(2)}) copy-start(s32[1,1024]{1,0:T(1,128)} %user_degree_hbm.1) | copy-start | bytes 12292
  1.4 2.2 %copy-start = (s32[1,1,64,128,128]{4,3,2,1,0:T(8,128)S(1)}, s32[1,1,64,128,128]{4,3,2,1,0:T(8,128)}, u32[]{:S(2)}) copy-start(s32[1,1,64,128,128]{4,3,2,1,0:T(8,128)} %param.15) | copy-start | bytes 12582916
  3.6 0.7 copy-start.7
  4.2 0.7 copy-start.8
  4.9 1.8 %copy-start.1 = (bf16[1,1024,256]{2,1,0:T(8,128)(2,1)S(1)}, bf16[1,1024,256]{2,1,0:T(8,128)(2,1)}, u32[]{:S(2)}) copy-start(bf16[1,1024,256]{2,1,0:T(8,128)(2,1)} %param.11) | copy-start | bytes 1572868
  4.9 1.8 %copy-start.2 = (bf16[1,1,128,256]{3,2,1,0:T(8,128)(2,1)S(1)}, bf16[1,1,128,256]{3,2,1,0:T(8,128)(2,1)}, u32[]{:S(2)}) copy-start(bf16[1,1,128,256]{3,2,1,0:T(8,128)(2,1)} %param.12) | copy-start | bytes 196612

commit v4 on v3

--- a/solution.py
+++ b/solution.py
@@ -246,8 +246,8 @@
         for by, later in ((2, 1), (1, 3), (3, 0)):
             sibling_part(r, term, later)
             own_part(r, term, by)
-            q_send(r, (by,), (2, 1))
-        q_send(r, (2, 1, 3), (3, 0))
+            q_send(r, (by,), (2, 1, 3))
+        q_send(r, (2, 1, 3), (0,))
         own_part(r, term, 0)
 
     def sum_q(r, rel):

time: 146 us -> 143 us (0.979); the launches traced: 144 us -> 143 us
  no operation moved by 1% of the time
where the time goes in v4:
time: 143 us
  Pallas kernels  136 us (95%)
  local copies, waits for them, and re-layouts  3.52 us (2%)
  other arithmetic  1.71 us (1%)
  between operations  1.44 us (1%)
    pallas_call x1, Pallas kernels, main(): pl.pallas_call(main_kernel, out_shape=(jax.ShapeDtypeStruct((rows_u, widt...  134 us
    unnamed x20, local copies, waits for them, and re-layouts  3.52 us

profile of v4, /device:TPU:0, one launch (start us, length us, event | category | flops | bytes accessed | tf_op | source)
XLA Modules:
  0.0 142.6 jit_solution(6857219339030248873)
XLA Ops:
  0.6 0.0 copy-start.6
  0.6 0.0 copy-start.5
  0.7 0.0 copy-start.4
  0.7 0.0 copy-start.9
  0.7 0.0 copy-start.3
  1.4 0.0 copy-start
  1.4 2.2 %copy-done = s32[1,1,64,128,128]{4,3,2,1,0:T(8,128)S(1)} copy-done((s32[1,1,64,128,128]{4,3,2,1,0:T(8,128)S(1)}, s32[1,1,64,128,128]{4,3,2,1,0:T(8,128)}, u32[]{:S(2)}) %copy-start) | copy-done | bytes 4194328
  3.6 0.0 copy-start.7
  3.6 0.7 copy-done.7
  4.2 0.0 copy-start.8
  4.2 0.7 copy-done.8
  4.9 0.0 copy-start.1
  4.9 0.0 copy-start.2
  4.9 1.6 %build.1.r_mat = bf16[2,1024,2048]{2,1,0:T(8,128)(2,1)S(1)} custom-call(s32[1,1]{1,0:T(1,128)S(6)} %copy.13.count_hbm, s32[1,64]{1,0:T(1,128)S(1)} %bitcast.20, s32[1,64]{1,0:T(1,128)S(1)} %bitcast.21, s32[64,128,128]{2,1,0:T(8,128)S(1)} %bitcast.14), custom_call_target="tpu_custom_call" | custom-call | tf_op jit(solution)/shard_map/build/pallas_call | solution.py:76
  6.5 0.0 copy-done.6
  6.5 0.0 copy-done.5
  6.5 0.0 copy-done.4
  6.6 0.0 copy-done.9
  6.6 0.0 copy-done.3
  6.6 0.0 copy-done.1
  6.6 0.0 copy-done.2
  6.6 134.3 %propagate.1 = (bf16[1024,256]{1,0:T(8,128)(2,1)S(1)}, f32[128,256]{1,0:T(8,128)S(1)}) custom-call(bf16[1024,256]{1,0:T(8,128)(2,1)S(1)} %bitcast.15, bf16[128,256]{1,0:T(8,128)(2,1)S(1)} %bitcast.16, s32[1,1024]{1,0:T(1,128)S(1)} %copy-done.3, s32[1,128]{1,0:T(1,128)S(1)} %bitcast.22, s32[1,256]{1,0:T(1,128)S(1)} %bitcast.17, s32[1,256]{1,0:T(1,128)S(1)} %bitcast.18, ...), custom_call_target="tpu_custom_call" | custom-call | tf_op jit(solution)/shard_map/propagate/pallas_call | solution.py:560
  140.9 0.7 multiply_bitcast_fusion
  141.6 1.0 bitcast_convert_fusion
Async XLA Ops:
  0.6 5.9 %copy-start.6 = (s32[1,1,256]{2,1,0:T(1,128)S(1)}, s32[1,1,256]{2,1,0:T(1,128)}, u32[]{:S(2)}) copy-start(s32[1,1,256]{2,1,0:T(1,128)} %param.21) | copy-start | bytes 3076
  0.6 5.9 %copy-start.5 = (s32[1,1,256]{2,1,0:T(1,128)S(1)}, s32[1,1,256]{2,1,0:T(1,128)}, u32[]{:S(2)}) copy-start(s32[1,1,256]{2,1,0:T(1,128)} %param.20) | copy-start | bytes 3076
  0.7 5.9 %copy-start.4 = (s32[1,1,256]{2,1,0:T(1,128)S(1)}, s32[1,1,256]{2,1,0:T(1,128)}, u32[]{:S(2)}) copy-start(s32[1,1,256]{2,1,0:T(1,128)} %param.19) | copy-start | bytes 3076
  0.7 5.9 %copy-start.9 = (s32[1,1,128]{2,1,0:T(1,128)S(1)}, s32[1,1,128]{2,1,0:T(1,128)}, u32[]{:S(2)}) copy-start(s32[1,1,128]{2,1,0:T(1,128)} %param.14) | copy-start | bytes 1540
  0.7 5.9 %copy-start.3 = (s32[1,1024]{1,0:T(1,128)S(1)}, s32[1,1024]{1,0:T(1,128)}, u32[]{:S(2)}) copy-start(s32[1,1024]{1,0:T(1,128)} %user_degree_hbm.1) | copy-start | bytes 12292
  1.4 2.2 %copy-start = (s32[1,1,64,128,128]{4,3,2,1,0:T(8,128)S(1)}, s32[1,1,64,128,128]{4,3,2,1,0:T(8,128)}, u32[]{:S(2)}) copy-start(s32[1,1,64,128,128]{4,3,2,1,0:T(8,128)} %param.15) | copy-start | bytes 12582916
  3.6 0.7 copy-start.7
  4.2 0.7 copy-start.8
  4.9 1.7 %copy-start.1 = (bf16[1,1024,256]{2,1,0:T(8,128)(2,1)S(1)}, bf16[1,1024,256]{2,1,0:T(8,128)(2,1)}, u32[]{:S(2)}) copy-start(bf16[1,1024,256]{2,1,0:T(8,128)(2,1)} %param.11) | copy-start | bytes 1572868
  4.9 1.7 %copy-start.2 = (bf16[1,1,128,256]{3,2,1,0:T(8,128)(2,1)S(1)}, bf16[1,1,128,256]{3,2,1,0:T(8,128)(2,1)}, u32[]{:S(2)}) copy-start(bf16[1,1,128,256]{3,2,1,0:T(8,128)(2,1)} %param.12) | copy-start | bytes 196612

commit v5 on v4

--- a/solution.py
+++ b/solution.py
@@ -433,8 +433,8 @@
     sum_make(1, item_term(1))
     gather_q(1)
     users_first(1)
+    users_last(1)
     sum_p(1)
-    users_last(1)
     forward_item(1, sum_end(1))
     user_turn(1, 0, forward_user)
     user_turn(1, 1, forward_user)

time: 143 us -> 143 us (level)
  no operation moved by 1% of the time
where the time goes in v5:
time: 143 us; the launch traced here: 142 us
  Pallas kernels  135 us (94%)
  local copies, waits for them, and re-layouts  3.52 us (2%)
  other arithmetic  1.71 us (1%)
  between operations  1.44 us (1%)
    pallas_call x1, Pallas kernels, main(): pl.pallas_call(main_kernel, out_shape=(jax.ShapeDtypeStruct((rows_u, widt...  134 us
    unnamed x20, local copies, waits for them, and re-layouts  3.52 us

profile of v5, /device:TPU:0, one launch (start us, length us, event | category | flops | bytes accessed | tf_op | source)
XLA Modules:
  0.0 142.2 jit_solution(6822435355651632214)
XLA Ops:
  0.6 0.0 copy-start.6
  0.6 0.0 copy-start.5
  0.7 0.0 copy-start.4
  0.7 0.0 copy-start.9
  0.7 0.0 copy-start.3
  1.4 0.0 copy-start
  1.4 2.2 %copy-done = s32[1,1,64,128,128]{4,3,2,1,0:T(8,128)S(1)} copy-done((s32[1,1,64,128,128]{4,3,2,1,0:T(8,128)S(1)}, s32[1,1,64,128,128]{4,3,2,1,0:T(8,128)}, u32[]{:S(2)}) %copy-start) | copy-done | bytes 4194328
  3.6 0.0 copy-start.7
  3.6 0.7 copy-done.7
  4.2 0.0 copy-start.8
  4.2 0.7 copy-done.8
  4.9 0.0 copy-start.1
  4.9 0.0 copy-start.2
  4.9 1.7 %build.1.r_mat = bf16[2,1024,2048]{2,1,0:T(8,128)(2,1)S(1)} custom-call(s32[1,1]{1,0:T(1,128)S(6)} %copy.13.count_hbm, s32[1,64]{1,0:T(1,128)S(1)} %bitcast.20, s32[1,64]{1,0:T(1,128)S(1)} %bitcast.21, s32[64,128,128]{2,1,0:T(8,128)S(1)} %bitcast.14), custom_call_target="tpu_custom_call" | custom-call | tf_op jit(solution)/shard_map/build/pallas_call | solution.py:76
  6.6 0.0 copy-done.6
  6.6 0.0 copy-done.5
  6.6 0.0 copy-done.4
  6.6 0.0 copy-done.9
  6.6 0.0 copy-done.3
  6.6 0.0 copy-done.1
  6.6 0.0 copy-done.2
  6.6 133.8 %propagate.1 = (bf16[1024,256]{1,0:T(8,128)(2,1)S(1)}, f32[128,256]{1,0:T(8,128)S(1)}) custom-call(bf16[1024,256]{1,0:T(8,128)(2,1)S(1)} %bitcast.15, bf16[128,256]{1,0:T(8,128)(2,1)S(1)} %bitcast.16, s32[1,1024]{1,0:T(1,128)S(1)} %copy-done.3, s32[1,128]{1,0:T(1,128)S(1)} %bitcast.22, s32[1,256]{1,0:T(1,128)S(1)} %bitcast.17, s32[1,256]{1,0:T(1,128)S(1)} %bitcast.18, ...), custom_call_target="tpu_custom_call" | custom-call | tf_op jit(solution)/shard_map/propagate/pallas_call | solution.py:560
  140.4 0.7 multiply_bitcast_fusion
  141.1 1.0 bitcast_convert_fusion
Async XLA Ops:
  0.6 5.9 %copy-start.6 = (s32[1,1,256]{2,1,0:T(1,128)S(1)}, s32[1,1,256]{2,1,0:T(1,128)}, u32[]{:S(2)}) copy-start(s32[1,1,256]{2,1,0:T(1,128)} %param.21) | copy-start | bytes 3076
  0.6 5.9 %copy-start.5 = (s32[1,1,256]{2,1,0:T(1,128)S(1)}, s32[1,1,256]{2,1,0:T(1,128)}, u32[]{:S(2)}) copy-start(s32[1,1,256]{2,1,0:T(1,128)} %param.20) | copy-start | bytes 3076
  0.7 5.9 %copy-start.4 = (s32[1,1,256]{2,1,0:T(1,128)S(1)}, s32[1,1,256]{2,1,0:T(1,128)}, u32[]{:S(2)}) copy-start(s32[1,1,256]{2,1,0:T(1,128)} %param.19) | copy-start | bytes 3076
  0.7 5.9 %copy-start.9 = (s32[1,1,128]{2,1,0:T(1,128)S(1)}, s32[1,1,128]{2,1,0:T(1,128)}, u32[]{:S(2)}) copy-start(s32[1,1,128]{2,1,0:T(1,128)} %param.14) | copy-start | bytes 1540
  0.7 5.9 %copy-start.3 = (s32[1,1024]{1,0:T(1,128)S(1)}, s32[1,1024]{1,0:T(1,128)}, u32[]{:S(2)}) copy-start(s32[1,1024]{1,0:T(1,128)} %user_degree_hbm.1) | copy-start | bytes 12292
  1.4 2.2 %copy-start = (s32[1,1,64,128,128]{4,3,2,1,0:T(8,128)S(1)}, s32[1,1,64,128,128]{4,3,2,1,0:T(8,128)}, u32[]{:S(2)}) copy-start(s32[1,1,64,128,128]{4,3,2,1,0:T(8,128)} %param.15) | copy-start | bytes 12582916
  3.6 0.7 copy-start.7
  4.2 0.7 copy-start.8
  4.9 1.7 %copy-start.1 = (bf16[1,1024,256]{2,1,0:T(8,128)(2,1)S(1)}, bf16[1,1024,256]{2,1,0:T(8,128)(2,1)}, u32[]{:S(2)}) copy-start(bf16[1,1024,256]{2,1,0:T(8,128)(2,1)} %param.11) | copy-start | bytes 1572868
  4.9 1.7 %copy-start.2 = (bf16[1,1,128,256]{3,2,1,0:T(8,128)(2,1)S(1)}, bf16[1,1,128,256]{3,2,1,0:T(8,128)(2,1)}, u32[]{:S(2)}) copy-start(bf16[1,1,128,256]{3,2,1,0:T(8,128)(2,1)} %param.12) | copy-start | bytes 196612
